TPU v7x, 128 devices: a whole 4x4x4 slice. The times are simulated.
128 devices in a mesh: src: 16 (over y, z), win: 8 (over x, core).
Axes of the slice: x: 4, y: 4, z: 4, core: 2. Of those that a mesh axis runs over, the one named last changes fastest.
Arguments:
- src_design: float32 [65536, 5, 128], P(('src', 'win')), may hold values from -6 to 6
- att_comp: float32 [65536, 4, 128], P(('src', 'win')), may hold values from -6 to 6
- spline_phase: float32 [65536, 128], P(('src', 'win')), may hold values from 0 to 1
- knot_offset: int32 [65536, 128], P(('src', 'win')), may hold values from 0 to 60
- obs_weight: float32 [65536, 128], P(('src', 'win')), may hold values from 9.765625e-05 to 0.0009765625
- residual: float32 [65536, 128], P(('src', 'win')), may hold values from -220 to 220
- block_source: int32 [65536], P(('src', 'win')), may hold values from 0 to 4095, as said below
- block_window: int32 [65536], P(('src', 'win')), may hold values from 0 to 255, as said below
- send_list: int32 [2048, 64], P(('src', 'win')), may hold values from 0 to 511, as said below
- send_count: int32 [2048], P(('src', 'win')), may hold values from 0 to 64, as said below
Outputs:
- source_step: float32 [5, 4096], P(None, 'src')
- attitude_step: float32 [256, 256], P(('src', 'win'))
- final_residual: float32 [65536, 128], P(('src', 'win'))
Inputs may be any that keep to these rules, and one draw needn't show every extreme that they name: `block_source`: Non-decreasing along the blocks of each device; the device at src index i names only sources i * 256 to (i + 1) * 256 - 1. `block_window`: window W is owned by the device whose flat index in src+win order is W // 2; every block names a window owned by a device of its own win index. `send_list`: row k of a device's lists names, in increasing order and as indices 0 to 511 into that device's blocks, its blocks whose windows the device at src index k of its win column owns; every block is named exactly once among the valid entries; entries past the count are 0. `send_count`: the counts of one device sum to 512; in every draw some owner of each win column receives exactly 64 blocks from every device of that column.
All inputs are finite; a program needn't handle non-finite values.
Results may differ from a plain program's by a relative error of at most 0.0003.
Values sent between devices are 32-bit elements; how exact they have to be, the bound alone decides.
No kernel may reach another device: no remote copies, remote signals or barrier semaphores. Data moves between devices by JAX's collectives and lax.ppermute only.
A program may use at most 192 MiB of HBM per device.

v0:
```python
import jax
import jax.numpy as jnp
from jax import lax
from jax.sharding import PartitionSpec as P

OBS = 128
KNOTS = 64
WIN_SUB = 2
BLK_DEV = 512
SRC_DEV = 256


def spline_weights(phase):
    square = phase * phase
    cube = square * phase
    rest = 1.0 - phase
    return [
        rest * rest * rest / 6.0,
        (3.0 * cube - 6.0 * square + 4.0) / 6.0,
        (-3.0 * cube + 3.0 * square + 3.0 * phase + 1.0) / 6.0,
        cube / 6.0,
    ]


def group_terms(phase, comps, weight, resid_one):
    count = phase.shape[0]
    spline = spline_weights(phase)
    pairs = (comps[:, :, None, :] * comps[:, None, :, :]).reshape(count, 16, OBS)
    weighted_pairs = weight[:, None, :] * pairs
    products = []
    for spacing in range(4):
        for first in range(4 - spacing):
            products.append(spline[first] * spline[first + spacing])
    spline_pairs = jnp.stack(products, axis=1)
    pair_terms = (spline_pairs[:, :, None, :] * weighted_pairs[:, None, :, :]).reshape(
        count, 160, OBS
    )
    weighted_resid = weight * resid_one
    spline_all = jnp.stack(spline, axis=1) * weighted_resid[:, None, :]
    right_terms = (spline_all[:, :, None, :] * comps[:, None, :, :]).reshape(count, 16, OBS)
    return (pair_terms, right_terms)


def shift_knots(values, amount):
    if amount == 0:
        return values
    padding = jnp.zeros_like(values[:, :, :amount])
    return jnp.concatenate([padding, values[:, :, :-amount]], axis=2)


def fold_bands(totals):
    count = totals.shape[0]
    totals = totals.reshape(count, 176, KNOTS)
    pieces = []
    slot_index = 0
    for spacing in range(4):
        band = jnp.zeros((count, 16, KNOTS), jnp.float32)
        for first in range(4 - spacing):
            band = band + shift_knots(totals[:, slot_index * 16 : (slot_index + 1) * 16], first)
            slot_index += 1
        pieces.append(band)
    right = jnp.zeros((count, 4, KNOTS), jnp.float32)
    for first in range(4):
        right = right + shift_knots(totals[:, 160 + first * 4 : 164 + first * 4], first)
    pieces.append(right)
    return jnp.concatenate(pieces, axis=1).reshape(count, 68 * KNOTS)


def solve_folded(folded, prior):
    count = folded.shape[0]
    folded = folded.reshape(count, 68, KNOTS).transpose(0, 2, 1)
    bands = [
        folded[:, :, spacing * 16 : (spacing + 1) * 16].reshape(count, KNOTS, 4, 4)
        for spacing in range(4)
    ]
    right = folded[:, :, 64:68].reshape(count, KNOTS * 4)
    dense = jnp.zeros((count, KNOTS, 4, KNOTS, 4), jnp.float32)
    for spacing in range(4):
        stepper = jnp.eye(KNOTS, k=spacing, dtype=jnp.float32)
        dense = dense + bands[spacing][:, :, :, None, :] * stepper[None, :, None, :, None]
        if spacing > 0:
            dense = (
                dense
                + bands[spacing].transpose(0, 3, 1, 2)[:, None] * stepper.T[None, :, None, :, None]
            )
    normal = (
        dense.reshape(count, KNOTS * 4, KNOTS * 4)
        + prior * jnp.eye(KNOTS * 4, dtype=jnp.float32)[None]
    )
    factor = jnp.linalg.cholesky(normal)
    return jax.scipy.linalg.cho_solve((factor, True), right[:, :, None])[:, :, 0]


def source_stats(design, weight, resid):
    weighted = design * weight[:, None, :]
    cross = jnp.einsum("bpo,bqo->bpq", weighted, design, precision=lax.Precision.HIGHEST)
    right = jnp.einsum("bpo,bo->bp", weighted, resid, precision=lax.Precision.HIGHEST)
    return jnp.concatenate([cross.reshape(design.shape[0], 25), right], axis=1)


def solve_five(totals):
    factor = {}
    for across in range(5):
        for within in range(across + 1):
            entry = totals[across * 5 + within]
            if across == within:
                entry = entry + 1.0
            for before in range(within):
                entry = entry - factor[across, before] * factor[within, before]
            if across == within:
                factor[across, within] = jnp.sqrt(entry)
            else:
                factor[across, within] = entry / factor[within, within]
    forward = []
    for across in range(5):
        entry = totals[25 + across]
        for before in range(across):
            entry = entry - factor[across, before] * forward[before]
        forward.append(entry / factor[across, across])
    backward = [None] * 5
    for across in range(4, -1, -1):
        entry = forward[across]
        for later in range(across + 1, 5):
            entry = entry - factor[later, across] * backward[later]
        backward[across] = entry / factor[across, across]
    return jnp.stack(backward, axis=0)


def owner_partials(phase, comps, weight, resid_one, knots, subs):
    count = phase.shape[0]
    group = min(64, count)
    turns = count // group
    columns = WIN_SUB * KNOTS

    def one_group(carry, pieces):
        phase_g, comps_g, weight_g, resid_g, knots_g, subs_g = pieces
        pair_terms, right_terms = group_terms(phase_g, comps_g, weight_g, resid_g)
        target = subs_g[:, None] * KNOTS + knots_g
        target_hot = (target[:, :, None] == jnp.arange(columns)[None, None, :]).astype(jnp.float32)
        pair_sum = jnp.einsum(
            "gfo,goj->fj", pair_terms, target_hot, precision=lax.Precision.HIGHEST
        )
        right_sum = jnp.einsum(
            "gfo,goj->fj", right_terms, target_hot, precision=lax.Precision.HIGHEST
        )
        return ((carry[0] + pair_sum, carry[1] + right_sum), None)

    pieces = (
        phase.reshape(turns, group, OBS),
        comps.reshape(turns, group, 4, OBS),
        weight.reshape(turns, group, OBS),
        resid_one.reshape(turns, group, OBS),
        knots.reshape(turns, group, OBS),
        subs.reshape(turns, group),
    )
    start = (jnp.zeros((160, columns), jnp.float32), jnp.zeros((16, columns), jnp.float32))
    sums, unused = lax.scan(one_group, start, pieces)
    joined = jnp.concatenate([sums[0], sums[1]], axis=0).reshape(176, WIN_SUB, KNOTS)
    return joined.transpose(1, 0, 2).reshape(WIN_SUB, 176 * KNOTS)


def attitude_correction(panel_rows, knots, phase, comps):
    count = panel_rows.shape[0]
    grid = jnp.concatenate(
        [panel_rows.reshape(count, KNOTS, 4), jnp.zeros((count, 3, 4), jnp.float32)], axis=1
    )
    stacked = jnp.concatenate([grid[:, first : first + KNOTS] for first in range(4)], axis=2)
    knot_hot = (knots[:, :, None] == jnp.arange(KNOTS)[None, None, :]).astype(jnp.float32)
    picked = jnp.einsum("boj,bjf->bfo", knot_hot, stacked, precision=lax.Precision.HIGHEST)
    spline = spline_weights(phase)
    correction = jnp.zeros_like(phase)
    for first in range(4):
        summed = jnp.sum(comps * picked[:, first * 4 : first * 4 + 4], axis=1)
        correction = correction + spline[first] * summed
    return correction


def shards(
    src_design,
    att_comp,
    spline_phase,
    knot_offset,
    obs_weight,
    residual,
    block_source,
    block_window,
    send_list,
    send_count,
):
    n_win = lax.axis_size("win")
    capacity = send_list.shape[1]
    owners = send_list.shape[0]
    local_source = block_source - lax.axis_index("src") * SRC_DEV
    source_hot = (local_source[:, None] == jnp.arange(SRC_DEV)[None, :]).astype(jnp.float32)
    stats = source_stats(src_design, obs_weight, residual)
    totals = jnp.einsum("bf,bs->fs", stats, source_hot, precision=lax.Precision.HIGHEST)
    totals = lax.psum(totals, "win")
    source_step = solve_five(totals)
    per_block = jnp.einsum("fs,bs->bf", source_step, source_hot, precision=lax.Precision.HIGHEST)
    resid_one = residual - jnp.sum(src_design * per_block[:, :, None], axis=1)
    column_window = block_window // (n_win * WIN_SUB) * WIN_SUB + block_window % WIN_SUB
    obs_src = OBS * BLK_DEV * n_win // SRC_DEV
    obs_win = OBS * BLK_DEV // WIN_SUB
    prior = 0.005 * obs_win / obs_src
    slot_valid = jnp.arange(capacity)[None, :] < send_count[:, None]
    flat_list = send_list.reshape(-1)
    valid_flat = slot_valid.reshape(-1)
    valid_weight = obs_weight[flat_list] * valid_flat.astype(jnp.float32)[:, None]
    payload = jnp.concatenate(
        [
            spline_phase[flat_list][:, None],
            valid_weight[:, None],
            resid_one[flat_list][:, None],
            att_comp[flat_list],
        ],
        axis=1,
    )
    payload = payload.reshape(owners, capacity, 7, OBS)
    knots_out = knot_offset[flat_list].reshape(owners, capacity, OBS)
    subs_out = (block_window[flat_list] % WIN_SUB).reshape(owners, capacity)
    got_payload, got_knots, got_subs = (
        lax.all_to_all(payload, "src", split_axis=0, concat_axis=0, tiled=True),
        lax.all_to_all(knots_out, "src", split_axis=0, concat_axis=0, tiled=True),
        lax.all_to_all(subs_out, "src", split_axis=0, concat_axis=0, tiled=True),
    )
    got_payload = got_payload.reshape(owners * capacity, 7, OBS)
    got_knots = got_knots.reshape(owners * capacity, OBS)
    totals_att = owner_partials(
        got_payload[:, 0],
        got_payload[:, 3:7],
        got_payload[:, 1],
        got_payload[:, 2],
        got_knots,
        got_subs.reshape(-1),
    )
    attitude_step = solve_folded(fold_bands(totals_att), prior)
    panels = lax.all_gather(attitude_step, "src", axis=0, tiled=True)
    panel_rows = panels[column_window]
    correction = attitude_correction(panel_rows, knot_offset, spline_phase, att_comp)
    return (source_step, attitude_step, resid_one - correction)


def solution(mesh):
    return jax.shard_map(
        shards,
        mesh=mesh,
        in_specs=(
            P(("src", "win"), None, None),
            P(("src", "win"), None, None),
            P(("src", "win"), None),
            P(("src", "win"), None),
            P(("src", "win"), None),
            P(("src", "win"), None),
            P(("src", "win")),
            P(("src", "win")),
            P(("src", "win"), None),
            P(("src", "win")),
        ),
        out_specs=(P(None, "src"), P(("src", "win"), None), P(("src", "win"), None)),
        check_vma=False,
    )
```

profile of v0, /device:TPU:0, one launch (start us, length us, event | category | flops | bytes accessed | tf_op | source)
XLA Modules:
  0.0 787.5 jit_solution(14933603180917023108)
XLA Ops:
  8.5 8.2 %all-to-all-start.1 = ((s32[16,1,64]{2,1,0:T(1,128)}), s32[16,1,64]{2,1,0:T(1,128)}, u32[]{:S(2)}, u32[]{:S(2)}) async-start(s32[16,1,64]{2,1,0:T(1,128)} %and_select_fusion), calls=%async_computation.1 | async-start | bytes 16384 | tf_op jit(solution)/shard_map/all_to_all | solution.py:224
  33.6 25.9 %psum.7 = f32[30,256]{1,0:T(8,128)S(1)} all-reduce(f32[30,256]{1,0:T(8,128)S(1)} %fusion.39), channel_id=1, replica_groups=mesh['src'=16,'win'=8] {'win'}, use_global_device_ids=true, to_apply=%region_0.0 | all-reduce | flops 7680 | bytes 61440 | tf_op jit(solution)/shard_map/psum | solution.py:197
  63.5 7.9 %gather_fusion.3 = f32[1024,4,128]{2,1,0:T(4,128)} fusion(f32[512,4,128]{2,1,0:T(4,128)S(1)} %copy-done.8, s32[1024]{0:T(1024)S(1)} %broadcast_clamp_fusion), kind=kCustom, calls=%fused_computation.3 | custom fusion | bytes 4198400 | tf_op jit(solution)/shard_map/gather | solution.py:214
  97.2 8.3 %mul.1114 = f32[256,256]{1,0:T(8,128)S(1)} reshape(f32[64,4,64,4]{3,2,1,0:T(8,128)} %mul.1113) | data formatting | bytes 524288 | tf_op jit(solution)/shard_map/mul | solution.py:80
  110.2 8.3 %mul.1120 = f32[256,256]{1,0:T(8,128)S(1)} reshape(f32[64,4,64,4]{3,2,1,0:T(8,128)} %mul.1119) | data formatting | bytes 524288 | tf_op jit(solution)/shard_map/mul | solution.py:84
  123.3 8.3 %mul.1127 = f32[256,256]{1,0:T(8,128)S(1)} reshape(f32[64,4,64,4]{3,2,1,0:T(8,128)} %mul.1126) | data formatting | bytes 524288 | tf_op jit(solution)/shard_map/mul | solution.py:80
  136.2 8.3 %mul.1133 = f32[256,256]{1,0:T(8,128)S(1)} reshape(f32[64,4,64,4]{3,2,1,0:T(8,128)} %mul.1132) | data formatting | bytes 524288 | tf_op jit(solution)/shard_map/mul | solution.py:84
  149.3 8.3 %mul.1140 = f32[256,256]{1,0:T(8,128)S(1)} reshape(f32[64,4,64,4]{3,2,1,0:T(8,128)} %mul.1139) | data formatting | bytes 524288 | tf_op jit(solution)/shard_map/mul | solution.py:80
  162.2 19.5 %mul.1146 = f32[256,256]{1,0:T(8,128)S(1)} reshape(f32[64,4,64,4]{3,2,1,0:T(8,128)} %mul.1145) | data formatting | bytes 524288 | tf_op jit(solution)/shard_map/mul | solution.py:84
  186.4 8.3 %mul.1107 = f32[256,256]{1,0:T(8,128)S(1)} reshape(f32[64,4,64,4]{3,2,1,0:T(8,128)} %mul.1106) | data formatting | bytes 524288 | tf_op jit(solution)/shard_map/mul | solution.py:80
  214.3 250.8 %while.15 = (s32[]{:T(128)}, f32[160,128]{1,0:T(8,128)S(1)}, f32[16,128]{1,0:T(8,128)}, f32[16,64,128]{2,1,0:T(8,128)S(1)}, f32[16,64,128]{2,1,0:T(8,128)}, /*in...) while((s32[]{:T(128)}, f32[160,128]{1,0:T(8,128)S(1)}, ...), condition=%wide.region_3.4_spmd.clone, body=%wide.region_2.3_spmd.clone.sunk | while | flops 2218856448 | bytes 17449884 | solution.py:157
  474.9 15.0 %mul.1105 = f32[2,256,256]{2,1,0:T(8,128)S(1)} reshape(f32[2,64,4,64,4]{4,3,2,1,0:T(8,128)} %mul.1104) | data formatting | bytes 1048576 | tf_op jit(solution)/shard_map/mul | solution.py:80
  497.2 15.4 %mul.1112 = f32[2,256,256]{2,1,0:T(8,128)S(1)} reshape(f32[2,64,4,64,4]{4,3,2,1,0:T(8,128)} %mul.1111) | data formatting | bytes 1048576 | tf_op jit(solution)/shard_map/mul | solution.py:80
  520.9 15.0 %mul.1118 = f32[2,256,256]{2,1,0:T(8,128)S(1)} reshape(f32[2,64,4,64,4]{4,3,2,1,0:T(8,128)} %mul.1117) | data formatting | bytes 1048576 | tf_op jit(solution)/shard_map/mul | solution.py:84
  543.2 15.0 %mul.1125 = f32[2,256,256]{2,1,0:T(8,128)S(1)} reshape(f32[2,64,4,64,4]{4,3,2,1,0:T(8,128)} %mul.1124) | data formatting | bytes 1048576 | tf_op jit(solution)/shard_map/mul | solution.py:80
  566.5 15.2 %mul.1131 = f32[2,256,256]{2,1,0:T(8,128)S(1)} reshape(f32[2,64,4,64,4]{4,3,2,1,0:T(8,128)} %mul.1130) | data formatting | bytes 1048576 | tf_op jit(solution)/shard_map/mul | solution.py:84
  589.8 15.0 %mul.1138 = f32[2,256,256]{2,1,0:T(8,128)S(1)} reshape(f32[2,64,4,64,4]{4,3,2,1,0:T(8,128)} %mul.1137) | data formatting | bytes 1048576 | tf_op jit(solution)/shard_map/mul | solution.py:80
  613.9 15.0 %mul.1144 = f32[2,256,256]{2,1,0:T(8,128)S(1)} reshape(f32[2,64,4,64,4]{4,3,2,1,0:T(8,128)} %mul.1143) | data formatting | bytes 1048576 | tf_op jit(solution)/shard_map/mul | solution.py:84
  632.5 23.5 %custom-call.20 = f32[2,128,128]{2,1,0:T(8,128)S(1)} custom-call(f32[2,128,128]{2,1,0:T(8,128)S(1)} %cholesky.122), custom_call_target="Cholesky" | custom-call | tf_op jit(solution)/shard_map/jit(cholesky)/cholesky | solution.py:90
  656.0 19.9 %custom-call.21 = f32[2,1,128,128]{2,3,1,0:T(8,128)S(1)} custom-call(f32[2,1,128,128]{3,2,1,0:T(8,128)S(1)} %select_bitcast_fusion), custom_call_target="InvertDiagBlocksLowerTriangular" | custom-call | tf_op jit(solution)/shard_map/jit(cholesky)/cholesky | solution.py:90
  676.5 23.5 %custom-call.22 = f32[2,128,128]{2,1,0:T(8,128)S(1)} custom-call(f32[2,128,128]{2,1,0:T(8,128)S(1)} %convolution_subtract_fusion), custom_call_target="Cholesky" | custom-call | tf_op jit(solution)/shard_map/jit(cholesky)/cholesky | solution.py:90
  705.5 40.1 %custom-call.23 = f32[2,2,128,128]{2,3,1,0:T(8,128)S(1)} custom-call(f32[2,2,128,128]{3,2,1,0:T(8,128)} %bitcast.261), custom_call_target="InvertDiagBlocksLowerTriangular" | custom-call | tf_op jit(solution)/shard_map/jit(_cho_solve)/vmap()/triangular_solve | solution.py:91
  747.5 21.4 %all-gather = f32[32,256,1]{1,2,0:T(1,128)S(1)} all-gather(f32[2,256,1]{1,2,0:T(1,128)S(1)} %pad_maximum_fusion.2), channel_id=2, replica_groups=mesh['src'=16,'win'=8] {'src'}, dimensions={0}, use_global_device_ids=true | all-gather | bytes 34816 | tf_op jit(solution)/shard_map/all_gather | solution.py:237
  773.9 9.3 %fusion.19 = f32[512,16,128]{2,1,0:T(8,128)S(1)} fusion(s32[512,128]{1,0:T(8,128)S(1)} %copy-done.6, f32[512,64,4]{1,2,0:T(4,128)S(1)} %get-tuple-element.195, f32[512,64,4]{1,2,0:T(4,128)S(1)} %get-tuple-element.194, f32[512,64,4]{1,2,0:T(4,128)S(1)} %get-tuple-element.193, f32[512,64,4]{1,2,0:T(4,128)S(1)} %copy.480), kind=kOutput, calls=%fused_computation.57 | convolution fusion | flops 811073536 | bytes 6553600 | tf_op jit(solution)/shard_map/boj,bjf->bfo/dot_general | solution.py:169
  (566 shorter events, 434.4 us)
Async XLA Ops:
  0.6 16.0 %copy-start.5 = (f32[512,128]{1,0:T(8,128)S(1)}, f32[512,128]{1,0:T(8,128)}, u32[]{:S(2)}) copy-start(f32[512,128]{1,0:T(8,128)} %param.16) | copy-start | bytes 786436
  1.5 19.2 %copy-start.7 = (f32[512,5,128]{2,0,1:T(8,128)S(1)}, f32[512,5,128]{2,0,1:T(8,128)}, u32[]{:S(2)}) copy-start(f32[512,5,128]{2,0,1:T(8,128)} %param.12) | copy-start | bytes 3932164
  8.5 73.7 %all-to-all-start.1 = ((s32[16,1,64]{2,1,0:T(1,128)}), s32[16,1,64]{2,1,0:T(1,128)}, u32[]{:S(2)}, u32[]{:S(2)}) async-start(s32[16,1,64]{2,1,0:T(1,128)} %and_select_fusion), calls=%async_computation.1 | async-start | bytes 16384 | tf_op jit(solution)/shard_map/all_to_all | solution.py:224
  20.8 8.2 %copy-start.10 = (f32[512,128]{1,0:T(8,128)S(1)}, f32[512,128]{1,0:T(8,128)}, u32[]{:S(2)}) copy-start(f32[512,128]{1,0:T(8,128)} %param.17) | copy-start | bytes 786436
  27.0 6.2 copy-start.14
  59.5 4.0 copy-start.8
  59.6 0.6 copy-start.13
  60.7 10.8 %copy-start.1 = (f32[512,128]{1,0:T(8,128)}, f32[512,128]{1,0:T(8,128)S(1)}, u32[]{:S(2)}) copy-start(f32[512,128]{1,0:T(8,128)S(1)} %sub.412) | copy-start | bytes 786436
  63.5 9.7 %copy-start.15 = (s32[16]{0:T(128)S(1)}, s32[16]{0:T(128)}, u32[]{:S(2)}) copy-start(s32[16]{0:T(128)} %param.21) | copy-start | bytes 196
  63.5 9.8 %copy-start.3 = (f32[512,128]{1,0:T(8,128)S(1)}, f32[512,128]{1,0:T(8,128)}, u32[]{:S(2)}) copy-start(f32[512,128]{1,0:T(8,128)} %param.14) | copy-start | bytes 786436
  82.2 7.1 copy-start.6
  82.2 114.7 %all-to-all-start = ((f32[16,64,7,128]{3,1,2,0:T(8,128)}), f32[16,64,7,128]{3,1,2,0:T(8,128)}, u32[]{:S(2)}, u32[]{:S(2)}) async-start(f32[16,64,7,128]{3,1,2,0:T(8,128)} %copy.444), calls=%async_computation | async-start | bytes 7340032 | tf_op jit(solution)/shard_map/all_to_all | solution.py:222
  186.4 9.2 %copy-start = (s32[512]{0:T(512)S(1)}, s32[512]{0:T(512)}, u32[]{:S(2)}) copy-start(s32[512]{0:T(512)} %param.19) | copy-start | bytes 6148
  196.9 17.4 %all-to-all-start.2 = ((s32[16,64,128]{2,1,0:T(8,128)}), s32[16,64,128]{2,1,0:T(8,128)}, u32[]{:S(2)}, u32[]{:S(2)}) async-start(s32[16,64,128]{2,1,0:T(8,128)} %bitcast.13), calls=%async_computation.2 | async-start | bytes 1048576 | tf_op jit(solution)/shard_map/all_to_all | solution.py:223
  632.1 68.1 %copy-start.11 = (pred[256,256]{1,0:T(8,128)(4,1)S(1)}, pred[256,256]{1,0:T(8,128)(4,1)}, u32[]{:S(2)}) copy-start(pred[256,256]{1,0:T(8,128)(4,1)} %iota_compare_fusion.17) | copy-start | bytes 196612
  632.1 68.2 %copy-start.16 = (s32[2]{0:T(128)S(1)}, s32[2]{0:T(128)}, u32[]{:S(2)}) copy-start(s32[2]{0:T(128)} %iota_multiply_fusion) | copy-start | bytes 28
  632.3 137.1 %copy-start.12 = (s32[1024]{0:T(1024)S(1)}, s32[1024]{0:T(1024)}, u32[]{:S(2)}) copy-start(s32[1024]{0:T(1024)} %pad_clamp_fusion) | copy-start | bytes 12292
  773.9 9.4 %copy-start.9 = (f32[512,4,128]{2,1,0:T(4,128)S(1)}, f32[512,4,128]{2,1,0:T(4,128)}, u32[]{:S(2)}) copy-start(f32[512,4,128]{2,1,0:T(4,128)} %param.13) | copy-start | bytes 3145732
  783.2 3.1 copy-start.2
  783.2 3.1 copy-start.4
where the time goes:
time: 801 us; the launch traced here: 788 us
  local copies, waits for them, and re-layouts  336 us (42%)
  other arithmetic  212 us (26%)
  matrix products  161 us (20%)
  blocking collectives  47.2 us (6%)
  starting transfers between devices  22.5 us (3%)
    mul x28, local copies, waits for them, and re-layouts, solve_folded(): bands[spacing][:, :, :, None, :] * stepper[None, :, None, :, None]  142 us
    mul x18, local copies, waits for them, and re-layouts, solve_folded(): bands[spacing].transpose(0, 3, 1, 2)[:, None]  120 us
    dot_general x16, matrix products, one_group(): jnp.einsum('gfo,goj->fj', pair_terms, target_hot, precision=lax.Precision...  89.5 us
    another operation x9, other arithmetic, solve_folded(): factor = jnp.linalg.cholesky(normal)  67 us
    dot_general x16, matrix products, one_group(): jnp.einsum('gfo,goj->fj', right_terms, target_hot, precision=lax.Precisio...  49.1 us
    mul x16, other arithmetic, group_terms(): spline_pairs[:, :, None, :] * weighted_pairs[:, None, :, :]  48.5 us
    another operation x7, other arithmetic, solve_folded(): jax.scipy.linalg.cho_solve((factor, True), right[:, :, None])[:, :, 0]  41.5 us
    psum x1, blocking collectives, shards(): totals = lax.psum(totals, 'win')  25.9 us
  transfers between devices with their start and end apart: 3, of which 1 were waited for; matrix products, arithmetic and copies ran while one was open for 19% of the time, Pallas kernels for 0%

commit v1 on v0

v1 whole, which is shorter than its diff:
```python
import jax
import jax.numpy as jnp
from jax import lax
from jax.experimental import pallas as pl
from jax.experimental.pallas import tpu as pltpu
from jax.sharding import PartitionSpec as P

OBS = 128
KNOTS = 64
WIN_SUB = 2
BLK_DEV = 512
SRC_DEV = 256
N_SRC = 16
N_COL = N_SRC * WIN_SUB
HALF = 30
PAIRS = [(p, q) for p in range(4) for q in range(p, 4)]
PAIR_ROWS = 8 * len(PAIRS)
RIGHT_ROWS = 16
ROWS = PAIR_ROWS + RIGHT_ROWS
STAT_ROWS = 24
F32 = jnp.float32
BF16 = jnp.bfloat16
NT = (((1,), (1,)), ((), ()))
SPLINE = [
    [1 / 6, 0.0, 0.0, 0.0],
    [4 / 6, 12 / 6, 6 / 6, 1 / 6],
    [1 / 6, 6 / 6, 12 / 6, 4 / 6],
    [0.0, 0.0, 0.0, 1 / 6],
]


def iota(shape, dim):
    return lax.broadcasted_iota(jnp.int32, shape, dim)


def split2(values):
    high = values.astype(BF16)
    return high, (values - high.astype(F32)).astype(BF16)


def split3(values):
    high = values.astype(BF16)
    rest = values - high.astype(F32)
    mid = rest.astype(BF16)
    return high, mid, (rest - mid.astype(F32)).astype(BF16)


def spline_weights(phase):
    square = phase * phase
    cube = square * phase
    rest = 1.0 - phase
    return [
        rest * rest * rest * (1.0 / 6.0),
        (3.0 * cube - 6.0 * square + 4.0) * (1.0 / 6.0),
        (-3.0 * cube + 3.0 * square + 3.0 * phase + 1.0) * (1.0 / 6.0),
        cube * (1.0 / 6.0),
    ]


def params(megabytes):
    return pltpu.CompilerParams(vmem_limit_bytes=megabytes * 1024 * 1024)


VMEM = pl.BlockSpec(memory_space=pltpu.VMEM)
SMEM = pl.BlockSpec(memory_space=pltpu.SMEM)


def stats_kernel(design_ref, weight_ref, resid_ref, source_ref, out_ref, sums_ref):
    rows = 32
    lane = iota((rows, OBS), 1)

    def one_group(group, carry):
        at = pl.ds(pl.multiple_of(group * rows, rows), rows)
        weight = weight_ref[at, :]
        design = [design_ref[p, at, :] for p in range(5)]
        resid = resid_ref[at, :]
        weighted = [weight * design[p] for p in range(5)]
        packed = jnp.zeros((rows, OBS), F32)
        slot = 0
        for p in range(5):
            for q in range(p + 1):
                total = jnp.sum(weighted[p] * design[q], axis=1, keepdims=True)
                packed = jnp.where(lane == slot, total, packed)
                slot += 1
        for p in range(5):
            total = jnp.sum(weighted[p] * resid, axis=1, keepdims=True)
            packed = jnp.where(lane == slot, total, packed)
            slot += 1
        sums_ref[at, :] = packed
        return carry

    lax.fori_loop(0, BLK_DEV // rows, one_group, 0)
    local = jnp.bitwise_and(source_ref[...], SRC_DEV - 1)
    hot = (iota((SRC_DEV, BLK_DEV), 0) == local).astype(F32).astype(BF16)
    total = jnp.zeros((SRC_DEV, OBS), F32)
    for piece in split3(sums_ref[...]):
        total = total + jnp.dot(hot, piece, preferred_element_type=F32)
    out_ref[...] = total.T[:STAT_ROWS]


def source_sums(design, weight, resid, source_row):
    return pl.pallas_call(
        stats_kernel,
        out_shape=jax.ShapeDtypeStruct((STAT_ROWS, SRC_DEV), F32),
        in_specs=[VMEM] * 4,
        out_specs=VMEM,
        scratch_shapes=[pltpu.VMEM((BLK_DEV, OBS), F32)],
        compiler_params=params(16),
        name="source_sums",
    )(design, weight, resid, source_row)


def column_window(window_ref, block):
    window = window_ref[block]
    return lax.shift_right_logical(window, 4) * 2 + jnp.bitwise_and(window, 1)


def normals_kernel(
    comp_ref,
    phase_ref,
    knot_ref,
    weight_ref,
    list_ref,
    count_ref,
    window_ref,
    out_ref,
    watt_ref,
    poly_ref,
    pair_ref,
    total_ref,
):
    named = jnp.zeros((16, BLK_DEV // 8), F32)
    capacity = list_ref.shape[1]
    slot = iota((1, capacity), 1)
    for owner in range(N_SRC):
        entry = jnp.where(slot < count_ref[owner], list_ref[owner : owner + 1, :], -1)
        group_hot = iota((BLK_DEV // 8, capacity), 0) == lax.shift_right_arithmetic(entry, 3)
        place_hot = iota((16, capacity), 0) == jnp.where(entry < 0, -1, jnp.bitwise_and(entry, 7))
        named = named + lax.dot_general(
            place_hot.astype(F32).astype(BF16),
            group_hot.astype(F32).astype(BF16),
            NT,
            preferred_element_type=F32,
        )
    named = jnp.concatenate([named[:8], jnp.zeros((8, OBS - BLK_DEV // 8), F32)], axis=1)

    def prepare(group, carry):
        at = pl.ds(pl.multiple_of(group * 8, 8), 8)
        phase = phase_ref[at, :]
        rest = 1.0 - phase
        up = [None, phase, phase * phase, None]
        down = [None, rest, rest * rest, None]
        up[3] = up[2] * phase
        down[3] = down[2] * rest
        poly = [
            down[3] * down[3],
            phase * (down[3] * down[2]),
            up[2] * (down[2] * down[2]),
            up[3] * down[3],
            (up[2] * up[2]) * down[2],
            (up[3] * up[2]) * rest,
            up[3] * up[3],
            jnp.zeros_like(phase),
        ]
        for k in range(8):
            poly_ref[pl.ds(group * 64 + k, 8, stride=8), :] = poly[k]
        times = jnp.take_along_axis(named, jnp.full((8, OBS), group, jnp.int32), axis=1)
        weight = weight_ref[at, :] * times
        watt_ref[at, :] = weight
        comps = [comp_ref[pl.ds(group * 32 + p, 8, stride=4), :] for p in range(4)]
        weighted = [weight * comps[p] for p in range(4)]
        for i, (p, q) in enumerate(PAIRS):
            pair_ref[i, at, :] = weighted[p] * comps[q]
        return carry

    lax.fori_loop(0, BLK_DEV // 8, prepare, 0, unroll=2)
    total_ref[...] = jnp.zeros_like(total_ref)
    knot_iota = iota((KNOTS, OBS), 0)
    unrolled = 16

    def one_group(group, carry):
        for i in range(unrolled):
            block = group * unrolled + i
            poly = poly_ref[pl.ds(pl.multiple_of(block * 8, 8), 8), :]
            terms = jnp.concatenate(
                [poly * pair_ref[n, pl.ds(block, 1), :] for n in range(len(PAIRS))], axis=0
            )
            high, low = split2(terms)
            hot = (knot_iota == knot_ref[pl.ds(block, 1), :]).astype(F32).astype(BF16)
            summed = lax.dot_general(
                jnp.concatenate([high, low], axis=1),
                jnp.concatenate([hot, hot], axis=1),
                NT,
                preferred_element_type=F32,
            )
            at = column_window(window_ref, block)
            total_ref[at] = total_ref[at] + summed
        return carry

    lax.fori_loop(0, BLK_DEV // unrolled, one_group, 0)
    for owner in range(N_SRC):
        out_ref[owner, :PAIR_ROWS, :] = jnp.concatenate(
            [total_ref[2 * owner], total_ref[2 * owner + 1]], axis=1
        )
        out_ref[owner, PAIR_ROWS:, :] = jnp.zeros((RIGHT_ROWS, OBS), F32)


def normal_sums(comps, phase, knots, weight, lists, counts, window):
    return pl.pallas_call(
        normals_kernel,
        out_shape=(
            jax.ShapeDtypeStruct((N_SRC, ROWS, OBS), F32),
            jax.ShapeDtypeStruct((BLK_DEV, OBS), F32),
        ),
        in_specs=[VMEM] * 5 + [SMEM] * 2,
        out_specs=(VMEM, VMEM),
        scratch_shapes=[
            pltpu.VMEM((BLK_DEV * 8, OBS), F32),
            pltpu.VMEM((len(PAIRS), BLK_DEV, OBS), F32),
            pltpu.VMEM((N_COL, PAIR_ROWS, KNOTS), F32),
        ],
        compiler_params=params(32),
        cost_estimate=pl.CostEstimate(flops=3_000_000_000, bytes_accessed=4_000_000, transcendentals=0),
        name="normal_sums",
    )(comps, phase, knots, weight, lists, counts, window)


def solve_five(totals):
    def entry_at(across, within):
        row = across * (across + 1) // 2 + within
        return totals[row : row + 1, :]

    factor = {}
    inverse = {}
    for across in range(5):
        for within in range(across + 1):
            entry = entry_at(across, within)
            if across == within:
                entry = entry + 1.0
            for before in range(within):
                entry = entry - factor[across, before] * factor[within, before]
            if across == within:
                inverse[across] = 1.0 / jnp.sqrt(entry)
            else:
                factor[across, within] = entry * inverse[within]
    forward = []
    for across in range(5):
        entry = totals[15 + across : 16 + across, :]
        for before in range(across):
            entry = entry - factor[across, before] * forward[before]
        forward.append(entry * inverse[across])
    backward = [None] * 5
    for across in range(4, -1, -1):
        entry = forward[across]
        for later in range(across + 1, 5):
            entry = entry - factor[later, across] * backward[later]
        backward[across] = entry * inverse[across]
    return backward


def rights_kernel(
    own_ref,
    near_ref,
    far_ref,
    cross_ref,
    design_ref,
    resid_ref,
    watt_ref,
    comp_ref,
    phase_ref,
    knot_ref,
    source_ref,
    window_ref,
    sums_in_ref,
    step_ref,
    first_ref,
    sums_ref,
    column_ref,
    term_ref,
    total_ref,
    right_ref,
    sem,
):
    totals = (own_ref[...] + near_ref[...]) + (far_ref[...] + cross_ref[...])
    step = solve_five(totals)
    for p in range(5):
        step_ref[p : p + 1, :] = step[p]
    stacked = jnp.concatenate(step + [jnp.zeros((3, SRC_DEV), F32)], axis=0)
    pieces = jnp.concatenate(list(split3(stacked)) + [jnp.zeros((8, SRC_DEV), BF16)], axis=0)
    local = jnp.bitwise_and(source_ref[...], SRC_DEV - 1)
    hot = (iota((SRC_DEV, BLK_DEV), 0) == local).astype(F32).astype(BF16)
    picked = jnp.dot(pieces, hot, preferred_element_type=F32)
    picked = picked[:8] + picked[8:16] + picked[16:24]
    column_ref[...] = jnp.concatenate([picked, jnp.zeros((OBS - 8, BLK_DEV), F32)], axis=0).T

    def prepare(group, carry):
        at = pl.ds(pl.multiple_of(group * 8, 8), 8)
        columns = column_ref[at, :]
        fitted = jnp.zeros((8, OBS), F32)
        for p in range(5):
            fitted = fitted + design_ref[p, at, :] * columns[:, p : p + 1]
        first = resid_ref[at, :] - fitted
        first_ref[at, :] = first
        weighted = watt_ref[at, :] * first
        spline = spline_weights(phase_ref[at, :])
        comps = [comp_ref[pl.ds(group * 32 + p, 8, stride=4), :] for p in range(4)]
        for m in range(4):
            scaled = weighted * spline[m]
            for p in range(4):
                term_ref[pl.ds(group * 128 + 4 * m + p, 8, stride=16), :] = scaled * comps[p]
        return carry

    lax.fori_loop(0, BLK_DEV // 8, prepare, 0, unroll=2)
    total_ref[...] = jnp.zeros_like(total_ref)
    knot_iota = iota((KNOTS, OBS), 0)
    unrolled = 16

    def one_group(group, carry):
        for i in range(unrolled):
            block = group * unrolled + i
            terms = term_ref[pl.ds(pl.multiple_of(block * 16, 16), 16), :]
            high, low = split2(terms)
            hot = (knot_iota == knot_ref[pl.ds(block, 1), :]).astype(F32).astype(BF16)
            summed = lax.dot_general(
                jnp.concatenate([high, low], axis=1),
                jnp.concatenate([hot, hot], axis=1),
                NT,
                preferred_element_type=F32,
            )
            at = column_window(window_ref, block)
            total_ref[at] = total_ref[at] + summed
        return carry

    lax.fori_loop(0, BLK_DEV // unrolled, one_group, 0)
    for owner in range(N_SRC):
        right_ref[owner] = jnp.concatenate([total_ref[2 * owner], total_ref[2 * owner + 1]], axis=1)
    copy = pltpu.make_async_copy(right_ref, sums_ref.at[:, PAIR_ROWS:ROWS, :], sem)
    copy.start()
    copy.wait()


def right_sums(parts, design, resid, watt, comps, phase, knots, source_row, window, sums):
    return pl.pallas_call(
        rights_kernel,
        out_shape=(
            jax.ShapeDtypeStruct((5, SRC_DEV), F32),
            jax.ShapeDtypeStruct((BLK_DEV, OBS), F32),
            jax.ShapeDtypeStruct((N_SRC, ROWS, OBS), F32),
        ),
        in_specs=[VMEM] * 11 + [SMEM, pl.BlockSpec(memory_space=pl.ANY)],
        out_specs=(VMEM, VMEM, pl.BlockSpec(memory_space=pl.ANY)),
        scratch_shapes=[
            pltpu.VMEM((BLK_DEV, OBS), F32),
            pltpu.VMEM((BLK_DEV * 16, OBS), F32),
            pltpu.VMEM((N_COL, RIGHT_ROWS, KNOTS), F32),
            pltpu.VMEM((N_SRC, RIGHT_ROWS, OBS), F32),
            pltpu.SemaphoreType.DMA,
        ],
        input_output_aliases={12: 2},
        compiler_params=params(32),
        name="right_sums",
    )(*parts, design, resid, watt, comps, phase, knots, source_row, window, sums)


def roll(values, amount, axis):
    size = values.shape[axis]
    return pltpu.roll(values, amount % size, axis) if amount % size else values


def convolved(first, second):
    out = [0.0] * 7
    for i in range(4):
        for j in range(4):
            out[i + j] += SPLINE[first][i] * SPLINE[second][j]
    return out


def solve_kernel(prior, got_ref, out_ref, sum_ref, work_ref):
    total = got_ref[0]
    for other in range(1, N_SRC):
        total = total + got_ref[other]
    sum_ref[...] = total
    lane8 = iota((8, OBS), 1)
    sublane8 = iota((8, OBS), 0)
    low_terms = [sum_ref[pl.ds(k, 8, stride=8), :] for k in range(7)]
    high_terms = [sum_ref[pl.ds(64 + k, 2, stride=8), :] for k in range(7)]
    bands = []
    for spacing in range(4):
        low = jnp.zeros((8, OBS), F32)
        high = jnp.zeros((2, OBS), F32)
        for first in range(4 - spacing):
            weights = convolved(first, first + spacing)
            low_slot = jnp.zeros((8, OBS), F32)
            high_slot = jnp.zeros((2, OBS), F32)
            for k in range(7):
                if weights[k] != 0.0:
                    low_slot = low_slot + weights[k] * low_terms[k]
                    high_slot = high_slot + weights[k] * high_terms[k]
            low = low + roll(low_slot, first, 1)
            high = high + roll(high_slot, first, 1)
        rows = [low[i : i + 1] for i in range(8)] + [high[i : i + 1] for i in range(2)]
        if spacing == 0:
            rows = [row + prior if PAIRS[i][0] == PAIRS[i][1] else row for i, row in enumerate(rows)]
        index = {}
        for i, (p, q) in enumerate(PAIRS):
            index[p, q] = index[q, p] = i
        full = [rows[index[p, q]] for p in range(4) for q in range(4)]
        bands.append([jnp.concatenate(full[:8], axis=0), jnp.concatenate(full[8:], axis=0)])
    right = sum_ref[PAIR_ROWS : PAIR_ROWS + 4, :]
    for first in range(1, 4):
        right = right + roll(sum_ref[PAIR_ROWS + 4 * first : PAIR_ROWS + 4 * first + 4, :], first, 1)
    right = jnp.concatenate([right, right], axis=0)

    place = jnp.bitwise_and(lane8, 31)
    window_at = jnp.bitwise_and(lane8, 64)
    is_down = jnp.bitwise_and(lane8, 32) != 0

    def arranged(values, spacing, base):
        step = place + base
        up_index = jnp.minimum(window_at + step, OBS - 1)
        down_index = jnp.maximum(window_at + KNOTS - 1 - step, 0)
        up = jnp.take_along_axis(roll(values, spacing, 1), up_index, axis=1)
        down = jnp.take_along_axis(values, down_index, axis=1)
        down = jnp.where(step - spacing >= HALF, 0.0, down)
        return jnp.where(is_down, down, up)

    stream = [arranged(bands[d][h], d, 0) for d in range(4) for h in range(2)] + [
        arranged(right, 0, 0)
    ]
    tail = [arranged(bands[d][h], d, 32) for d in range(4) for h in range(2)] + [
        arranged(right, 0, 32)
    ]
    lower = sublane8 < 4

    def insert(front, target, pieces, slot, present):
        def part(d, p, half):
            values = pieces[2 * d + p // 2]
            return values if p % 2 == half else roll(values, 4, 0)

        for d in range(1, present + 1):
            other = (slot - d) % 4
            for q in range(4):
                old = front[other * 4 + q]
                fresh = part(d, q, slot % 2)
                keep = lower if slot % 2 == 1 else jnp.logical_not(lower)
                old[slot // 2] = jnp.where(keep, old[slot // 2], fresh)
        for p in range(4):
            halves = []
            for h in range(2):
                both = []
                for spot in range(2):
                    d = (slot - (2 * h + spot)) % 4
                    both.append(part(d, p, spot) if d <= present else jnp.zeros((8, OBS), F32))
                halves.append(jnp.where(lower, both[0], both[1]))
            front[slot * 4 + p] = halves
        keep = lower if slot % 2 == 1 else jnp.logical_not(lower)
        target[slot // 2] = jnp.where(keep, target[slot // 2], pieces[8])

    def eliminate(front, target, slot, gone):
        for p in range(4):
            row = slot * 4 + p
            half, at = row // 8, row % 8
            column = front[row]
            inverse = 1.0 / column[half][at : at + 1, :]
            gone = gone | {row}
            for c in [c for c in range(16) if c not in gone] + [16]:
                values = target if c == 16 else front[c]
                factor = values[half][at : at + 1, :] * inverse
                for h in range(2):
                    values[h] = values[h] - column[h] * factor
                values[half] = jnp.where(sublane8 == at, factor, values[half])
        return gone

    def save(front, target, slot, step):
        for r in range(1, 4):
            for q in range(4):
                work_ref[step * 13 + (r - 1) * 4 + q] = front[(slot + r) % 4 * 4 + q][slot // 2]
        work_ref[step * 13 + 12] = target[slot // 2]

    zero = jnp.zeros((8, OBS), F32)
    front = [[zero, zero] for _ in range(16)]
    target = [zero, zero]
    for step in range(4):
        insert(front, target, stream, step, step)
        stream = [roll(values, -1, 1) for values in stream]

    def four_knots(turn, carry):
        front = [list(pair) for pair in carry[0]]
        target = list(carry[1])
        stream = list(carry[2])
        for slot in range(4):
            eliminate(front, target, slot, frozenset())
            save(front, target, slot, turn * 4 + slot)
            insert(front, target, stream, slot, 3)
            stream = [roll(values, -1, 1) for values in stream]
        return (front, target, stream)

    front, target, stream = lax.fori_loop(0, 7, four_knots, (front, target, stream))
    for slot in range(2):
        eliminate(front, target, slot, frozenset())
        save(front, target, slot, 28 + slot)
        insert(front, target, tail, slot, 3)
        tail = [roll(values, -1, 1) for values in tail]

    mirror = jnp.bitwise_xor(lane8, 32)

    def mirrored(values):
        return jnp.take_along_axis(roll(values, 4, 0), mirror, axis=1)

    front = [
        [front[a * 4 + p][h] + mirrored(front[(3 - a) * 4 + p][1 - h]) for h in range(2)]
        for a in range(4)
        for p in range(4)
    ]
    target = [target[h] + mirrored(target[1 - h]) for h in range(2)]
    gone = frozenset()
    for slot in (2, 3, 0, 1):
        gone = eliminate(front, target, slot, gone)

    first_lane = place == 0

    def emit(result, answer, slot):
        values = answer[slot // 2]
        values = values if slot % 2 == 0 else roll(values, 4, 0)
        return jnp.where(first_lane, values, roll(result, 1, 1))

    def back(answer, slot, step):
        half = slot // 2
        sums = [work_ref[step * 13 + 12], zero]
        for r in (3, 2, 1):
            other = (slot + r) % 4
            for q in range(4):
                at = other % 2 * 4 + q
                sums[q % 2] = sums[q % 2] - work_ref[step * 13 + (r - 1) * 4 + q] * (
                    answer[other // 2][at : at + 1, :]
                )
        fresh = sums[0] + sums[1]
        keep = lower if slot % 2 == 1 else jnp.logical_not(lower)
        answer[half] = jnp.where(keep, answer[half], fresh)

    answer = list(target)
    result = emit(zero, answer, 3)
    result = emit(result, answer, 2)
    for slot in (1, 0):
        back(answer, slot, 28 + slot)
        result = emit(result, answer, slot)

    def four_back(turn, carry):
        answer = list(carry[0])
        result = carry[1]
        for slot in (3, 2, 1, 0):
            back(answer, slot, (6 - turn) * 4 + slot)
            result = emit(result, answer, slot)
        return (answer, result)

    answer, result = lax.fori_loop(0, 7, four_back, (answer, result))
    knot = jnp.bitwise_and(lane8, KNOTS - 1)
    from_lane = jnp.where(knot < 32, lane8, window_at + 32 + KNOTS - 1 - knot)
    panel = jnp.take_along_axis(result, from_lane, axis=1)
    for owner in range(N_SRC):
        out_ref[owner] = panel


def solve_panels(got, prior):
    def body(*refs):
        solve_kernel(prior, *refs)

    return pl.pallas_call(
        body,
        out_shape=jax.ShapeDtypeStruct((N_SRC, 8, OBS), F32),
        in_specs=[VMEM],
        out_specs=VMEM,
        scratch_shapes=[
            pltpu.VMEM((ROWS, OBS), F32),
            pltpu.VMEM((HALF * 13, 8, OBS), F32),
        ],
        compiler_params=params(16),
        name="solve_panels",
    )(got)


def final_kernel(panel_ref, comp_ref, phase_ref, knot_ref, first_ref, window_ref, out_ref, table_ref):
    for owner in range(N_SRC):
        tile = panel_ref[owner]
        table_ref[owner * 16 : owner * 16 + 8, :] = tile
        table_ref[owner * 16 + 8 : owner * 16 + 16, :] = roll(tile, 64, 1)

    def one_group(group, carry):
        at = pl.ds(pl.multiple_of(group * 8, 8), 8)
        knots = knot_ref[at, :]
        spline = spline_weights(phase_ref[at, :])
        starts = [column_window(window_ref, group * 8 + i) * 8 for i in range(8)]
        correction = [jnp.zeros((8, OBS), F32) for _ in range(4)]
        for p in range(4):
            table = jnp.concatenate([table_ref[pl.ds(start + p, 1), :] for start in starts], axis=0)
            comps = comp_ref[pl.ds(group * 32 + p, 8, stride=4), :]
            for m in range(4):
                correction[m] = correction[m] + comps * jnp.take_along_axis(table, knots + m, axis=1)
        total = spline[0] * correction[0]
        for m in range(1, 4):
            total = total + spline[m] * correction[m]
        out_ref[at, :] = first_ref[at, :] - total
        return carry

    lax.fori_loop(0, BLK_DEV // 8, one_group, 0, unroll=4)


def final_residual(panels, comps, phase, knots, first, window):
    return pl.pallas_call(
        final_kernel,
        out_shape=jax.ShapeDtypeStruct((BLK_DEV, OBS), F32),
        in_specs=[VMEM] * 5 + [SMEM],
        out_specs=VMEM,
        scratch_shapes=[pltpu.VMEM((N_COL * 8, OBS), F32)],
        compiler_params=params(16),
        name="final_residual",
    )(panels, comps, phase, knots, first, window)


def shards(
    src_design,
    att_comp,
    spline_phase,
    knot_offset,
    obs_weight,
    residual,
    block_source,
    block_window,
    send_list,
    send_count,
):
    n_win = lax.axis_size("win")
    design = src_design.transpose(1, 0, 2)
    comps = att_comp.reshape(BLK_DEV * 4, OBS)
    source_row = block_source.reshape(1, BLK_DEV)
    obs_src = OBS * BLK_DEV * n_win // SRC_DEV
    obs_win = OBS * BLK_DEV // WIN_SUB
    prior = 0.005 * obs_win / obs_src

    def swap(values, bit):
        return lax.ppermute(values, "win", [(i, i ^ bit) for i in range(n_win)])

    stats = source_sums(design, obs_weight, residual, source_row)
    stats = stats + swap(stats, 1)
    parts = (stats, swap(stats, 2), swap(stats, 4), swap(stats, 6))
    sums, watt = normal_sums(
        comps, spline_phase, knot_offset, obs_weight, send_list, send_count, block_window
    )
    source_step, first, sums = right_sums(
        parts,
        design,
        residual,
        watt,
        comps,
        spline_phase,
        knot_offset,
        source_row,
        block_window,
        sums,
    )
    got = lax.all_to_all(sums, "src", split_axis=0, concat_axis=0, tiled=True)
    own_panels = solve_panels(got, prior)
    panels = lax.all_to_all(own_panels, "src", split_axis=0, concat_axis=0, tiled=True)
    attitude_step = (
        own_panels[0, :4].reshape(4, WIN_SUB, KNOTS).transpose(1, 2, 0).reshape(WIN_SUB, KNOTS * 4)
    )
    last = final_residual(panels, comps, spline_phase, knot_offset, first, block_window)
    return (source_step, attitude_step, last)


def solution(mesh):
    return jax.shard_map(
        shards,
        mesh=mesh,
        in_specs=(
            P(("src", "win"), None, None),
            P(("src", "win"), None, None),
            P(("src", "win"), None),
            P(("src", "win"), None),
            P(("src", "win"), None),
            P(("src", "win"), None),
            P(("src", "win")),
            P(("src", "win")),
            P(("src", "win"), None),
            P(("src", "win")),
        ),
        out_specs=(P(None, "src"), P(("src", "win"), None), P(("src", "win"), None)),
        check_vma=False,
    )
```

time: 801 us -> 85.9 us (0.11); the launches traced: 788 us -> 85.5 us
  local copies, waits for them, and re-layouts: 336 us -> 5.44 us
  other arithmetic: 212 us -> 0.01 us
  matrix products: 161 us -> 0 us
  Pallas kernels: 0 us -> 42.6 us
  blocking collectives: 47.2 us -> 21.5 us
  starting transfers between devices: 22.5 us -> 7.78 us
    mul x78 -> x0, local copies, waits for them, and re-layouts: 276 us -> none  [the longest x28 142 us: solve_folded(): bands[spacing][:, :, :, None, :] * stepper[None, :, None, :, None]]
    dot_general x37 -> x0, matrix products: 159 us -> none  [the longest x16 89.5 us: one_group(): jnp.einsum('gfo,goj->fj', pair_terms, target_hot, precision=lax.Precision...]
    another operation x32 -> x0, other arithmetic: 109 us -> none  [the longest x9 67 us: solve_folded(): factor = jnp.linalg.cholesky(normal)]
    mul x99 -> x0, other arithmetic: 78.5 us -> none  [the longest x16 48.5 us: group_terms(): spline_pairs[:, :, None, :] * weighted_pairs[:, None, :, :]]
    pallas_call x0 -> x5, Pallas kernels: none -> 42.6 us  [the longest x1 14.3 us: normal_sums(): pl.pallas_call(normals_kernel, out_shape=(jax.ShapeDtypeStruct((N_SRC, RO...]
    gather x10 -> x0, local copies, waits for them, and re-layouts: 33 us -> none  [the longest x2 9.67 us: shards(): att_comp[flat_list]]
    psum x1 -> x0, blocking collectives: 25.9 us -> none  [shards(): totals = lax.psum(totals, 'win')]
    all_to_all x0 -> x1, blocking collectives: none -> 21.5 us  [shards(): got = lax.all_to_all(sums, 'src', split_axis=0, concat_axis=0, tiled=True)]
  transfers between devices with their start and end apart: 3 -> 5, of which waited for: 1 -> 2; matrix products, arithmetic and copies ran while one was open for 19% -> 2% of each run, Pallas kernels for 0% -> 17%
where the time goes in v1:
time: 85.9 us; the launch traced here: 85.5 us
  Pallas kernels  42.6 us (50%)
  blocking collectives  21.5 us (25%)
  starting transfers between devices  7.78 us (9%)
  waiting for transfers between devices  7.36 us (9%)
  local copies, waits for them, and re-layouts  5.44 us (6%)
    all_to_all x1, blocking collectives, shards(): got = lax.all_to_all(sums, 'src', split_axis=0, concat_axis=0, tiled=True)  21.5 us
    pallas_call x1, Pallas kernels, normal_sums(): pl.pallas_call(normals_kernel, out_shape=(jax.ShapeDtypeStruct((N_SRC, RO...  14.3 us
    pallas_call x1, Pallas kernels, right_sums(): pl.pallas_call(rights_kernel, out_shape=(jax.ShapeDtypeStruct((5, SRC_DEV...  13.8 us
    all_to_all x1, waiting for transfers between devices, shards(): lax.all_to_all(own_panels, 'src', split_axis=0, concat_axis=0, tiled=True)  6.17 us
    pallas_call x1, Pallas kernels, solve_panels(): pl.pallas_call(body, out_shape=jax.ShapeDtypeStruct((N_SRC, 8, OBS), F32)...  6.03 us
    pallas_call x1, Pallas kernels, final_residual(): pl.pallas_call(final_kernel, out_shape=jax.ShapeDtypeStruct((BLK_DEV, OBS...  5.45 us
    ppermute x4, starting transfers between devices, swap(): return lax.ppermute(values, 'win', [(i, i ^ bit) for i in range(n_win)])  4.15 us
    unnamed x28, local copies, waits for them, and re-layouts  3.95 us
  transfers between devices with their start and end apart: 5, of which 2 were waited for; matrix products, arithmetic and copies ran while one was open for 2% of the time, Pallas kernels for 17%

profile of v1, /device:TPU:0, one launch (start us, length us, event | category | flops | bytes accessed | tf_op | source)
XLA Modules:
  0.0 85.5 jit_solution(10507860955161159700)
XLA Ops:
  0.7 0.0 copy-start
  0.7 1.3 %copy-done = f32[512,5,128]{2,0,1:T(8,128)S(1)} copy-done((f32[512,5,128]{2,0,1:T(8,128)S(1)}, f32[512,5,128]{2,0,1:T(8,128)}, u32[]{:S(2)}) %copy-start) | copy-done | bytes 1310744
  2.0 0.9 %copy-done.5 = f32[512,128]{1,0:T(8,128)S(1)} copy-done((f32[512,128]{1,0:T(8,128)S(1)}, f32[512,128]{1,0:T(8,128)}, u32[]{:S(2)}) %copy-start.5) | copy-done | bytes 262168
  2.9 0.9 %copy-done.7 = f32[512,128]{1,0:T(8,128)S(1)} copy-done((f32[512,128]{1,0:T(8,128)S(1)}, f32[512,128]{1,0:T(8,128)}, u32[]{:S(2)}) %copy-start.7) | copy-done | bytes 262168
  3.9 0.7 copy-done.10
  4.6 3.0 %source_sums.1 = f32[24,256]{1,0:T(8,128)S(1)} custom-call(f32[5,512,128]{2,1,0:T(8,128)S(1)} %bitcast.6, f32[512,128]{1,0:T(8,128)S(1)} %copy-done.7, f32[512,128]{1,0:T(8,128)S(1)} %copy-done.5, s32[1,512]{1,0:T(1,128)S(1)} %bitcast.11), custom_call_target="tpu_custom_call" | custom-call | tf_op jit(solution)/shard_map/source_sums/pallas_call | solution.py:102
  7.6 0.1 collective-permute-start
  7.7 1.2 %collective-permute-done = f32[24,256]{1,0:T(8,128)S(1)} collective-permute-done((f32[24,256]{1,0:T(8,128)S(1)}, f32[24,256]{1,0:T(8,128)S(1)}, u32[]{:S(2)}, u32[]{:S(2)}) %collective-permute-start) | collective-permute-done | bytes 24608 | tf_op jit(solution)/shard_map/ppermute | solution.py:641
  8.9 2.8 %collective-permute-start.3 = (f32[24,256]{1,0:T(8,128)S(1)}, f32[24,256]{1,0:T(8,128)S(1)}, u32[]{:S(2)}, u32[]{:S(2)}) collective-permute-start(f32[24,256]{1,0:T(8,128)S(1)} %add.3.own_ref), channel_id=1, source_target_pairs={{0,6},{1,7},{2,4},{3,5},{4,2},{5,3},{6,0},{7,1},{8,14},{9,15},{10,... | collective-permute-start | bytes 73736 | tf_op jit(solution)/shard_map/ppermute | solution.py:641
  11.7 0.8 collective-permute-start.2
  12.5 0.5 collective-permute-start.1
  13.0 0.0 copy-start.1
  13.0 0.0 copy-start.6
  13.0 0.0 copy-start.11
  13.0 14.3 %normal_sums.1 = (f32[16,96,128]{2,1,0:T(8,128)S(1)}, f32[512,128]{1,0:T(8,128)S(1)}) custom-call(f32[2048,128]{1,0:T(8,128)S(1)} %bitcast.8, f32[512,128]{1,0:T(8,128)S(1)} %copy-done.3, s32[512,128]{1,0:T(8,128)S(1)} %copy-done.4, f32[512,128]{1,0:T(8,128)S(1)} %copy-done.8, s32[16,64]{1,0:T(8,128)S(1)} %copy-done.12, s32[16]{0:T(128)S(1)} %copy-done.13, ...), custom_call_target="tpu_custom_call" | custom-call | flops 3000000000 | bytes 4000000 | tf_op jit(solution)/shard_map/normal_sums/pallas_call | solution.py:209
  27.4 13.8 %right_sums.1 = (f32[5,256]{1,0:T(8,128)}, f32[512,128]{1,0:T(8,128)S(1)}, f32[16,96,128]{2,1,0:T(8,128)S(1)}) custom-call(f32[24,256]{1,0:T(8,128)S(1)} %add.3.own_ref, f32[24,256]{1,0:T(8,128)S(1)} %collective-permute-done.1.near_ref, f32[24,256]{1,0:T(8,128)S(1)} %collective-permute-done.2.far_ref, ...), custom_call_target="tpu_custom_call", output_to_operand_aliasing={{2}: (12, {})} | custom-call | tf_op jit(solution)/shard_map/right_sums/pallas_call | solution.py:343
  41.2 21.5 %all_to_all.10.refs_0_ = f32[16,96,128]{2,1,0:T(8,128)S(1)} all-to-all(f32[16,96,128]{2,1,0:T(8,128)S(1)} %get-tuple-element.11), channel_id=1, replica_groups=mesh['src'=16,'win'=8] {'src'}, dimensions={0} | all-to-all | bytes 1572864 | tf_op jit(solution)/shard_map/all_to_all | solution.py:661
  62.7 6.0 %solve_panels.1 = f32[16,8,128]{2,1,0:T(8,128)} custom-call(f32[16,96,128]{2,1,0:T(8,128)S(1)} %all_to_all.10.refs_0_), custom_call_target="tpu_custom_call" | custom-call | tf_op jit(solution)/shard_map/solve_panels/pallas_call | solution.py:568
  68.8 3.6 %all-to-all-start.1 = ((f32[16,8,128]{2,1,0:T(8,128)}), f32[16,8,128]{2,1,0:T(8,128)S(1)}, u32[]{:S(2)}, u32[]{:S(2)}) async-start(f32[16,8,128]{2,1,0:T(8,128)} %solve_panels.1), calls=%async_computation.1 | async-start | bytes 131072 | tf_op jit(solution)/shard_map/all_to_all | solution.py:663
  72.4 0.7 slice.4
  73.1 0.1 copy.16
  73.2 0.7 reshape.17
  73.9 6.2 %all-to-all-done.1.panel_ref = f32[16,8,128]{2,1,0:T(8,128)S(1)} async-done(((f32[16,8,128]{2,1,0:T(8,128)}), f32[16,8,128]{2,1,0:T(8,128)S(1)}, u32[]{:S(2)}, u32[]{:S(2)}) %all-to-all-start.1) | async-done | bytes 65568 | tf_op jit(solution)/shard_map/all_to_all | solution.py:663
  80.1 5.4 %final_residual.1 = f32[512,128]{1,0:T(8,128)} custom-call(f32[16,8,128]{2,1,0:T(8,128)S(1)} %all-to-all-done.1.panel_ref, f32[2048,128]{1,0:T(8,128)S(1)} %bitcast.10, f32[512,128]{1,0:T(8,128)S(1)} %copy-done.3, s32[512,128]{1,0:T(8,128)S(1)} %copy-done.4, f32[512,128]{1,0:T(8,128)S(1)} %get-tuple-element.12.first_ref, s32[512]{0:T(512)S(1)} %copy-done.9), custom_call_target="tpu_custom_call" | custom-call | tf_op jit(solution)/shard_map/final_residual/pallas_call | solution.py:609
  (24 shorter events, 0.1 us)
Async XLA Ops:
  0.6 12.3 %copy-start.9 = (s32[512]{0:T(512)S(1)}, s32[512]{0:T(512)}, u32[]{:S(2)}) copy-start(s32[512]{0:T(512)} %window_ref.5) | copy-start | bytes 6148
  0.6 12.3 %copy-start.13 = (s32[16]{0:T(128)S(1)}, s32[16]{0:T(128)}, u32[]{:S(2)}) copy-start(s32[16]{0:T(128)} %count_ref.1) | copy-start | bytes 196
  0.7 1.3 %copy-start = (f32[512,5,128]{2,0,1:T(8,128)S(1)}, f32[512,5,128]{2,0,1:T(8,128)}, u32[]{:S(2)}) copy-start(f32[512,5,128]{2,0,1:T(8,128)} %param.10) | copy-start | bytes 3932164
  2.0 0.9 %copy-start.5 = (f32[512,128]{1,0:T(8,128)S(1)}, f32[512,128]{1,0:T(8,128)}, u32[]{:S(2)}) copy-start(f32[512,128]{1,0:T(8,128)} %resid_ref.3) | copy-start | bytes 786436
  2.9 0.9 %copy-start.7 = (f32[512,128]{1,0:T(8,128)S(1)}, f32[512,128]{1,0:T(8,128)}, u32[]{:S(2)}) copy-start(f32[512,128]{1,0:T(8,128)} %weight_ref.3) | copy-start | bytes 786436
  3.9 0.7 copy-start.10
  4.6 8.4 %copy-start.2 = (f32[512,4,128]{2,1,0:T(4,128)S(1)}, f32[512,4,128]{2,1,0:T(4,128)}, u32[]{:S(2)}) copy-start(f32[512,4,128]{2,1,0:T(4,128)} %param.11) | copy-start | bytes 3145732
  4.6 8.4 %copy-start.3 = (f32[512,128]{1,0:T(8,128)S(1)}, f32[512,128]{1,0:T(8,128)}, u32[]{:S(2)}) copy-start(f32[512,128]{1,0:T(8,128)} %phase_ref.5) | copy-start | bytes 786436
  4.6 8.4 %copy-start.4 = (s32[512,128]{1,0:T(8,128)S(1)}, s32[512,128]{1,0:T(8,128)}, u32[]{:S(2)}) copy-start(s32[512,128]{1,0:T(8,128)} %knot_ref.5) | copy-start | bytes 786436
  4.6 8.4 %copy-start.8 = (f32[512,128]{1,0:T(8,128)S(1)}, f32[512,128]{1,0:T(8,128)}, u32[]{:S(2)}) copy-start(f32[512,128]{1,0:T(8,128)} %weight_ref.3) | copy-start | bytes 786436
  4.6 8.4 %copy-start.12 = (s32[16,64]{1,0:T(8,128)S(1)}, s32[16,64]{1,0:T(8,128)}, u32[]{:S(2)}) copy-start(s32[16,64]{1,0:T(8,128)} %list_ref.1) | copy-start | bytes 12292
  7.6 1.2 %collective-permute-start = (f32[24,256]{1,0:T(8,128)S(1)}, f32[24,256]{1,0:T(8,128)S(1)}, u32[]{:S(2)}, u32[]{:S(2)}) collective-permute-start(f32[24,256]{1,0:T(8,128)S(1)} %source_sums.1), channel_id=1, source_target_pairs={{0,1},{1,0},{2,3},{3,2},{4,5},{5,4},{6,7},{7,6},{8,9},{9,8},{10,11... | collective-permute-start | bytes 73736 | tf_op jit(solution)/shard_map/ppermute | solution.py:641
  8.9 18.4 %collective-permute-start.3 = (f32[24,256]{1,0:T(8,128)S(1)}, f32[24,256]{1,0:T(8,128)S(1)}, u32[]{:S(2)}, u32[]{:S(2)}) collective-permute-start(f32[24,256]{1,0:T(8,128)S(1)} %add.3.own_ref), channel_id=1, source_target_pairs={{0,6},{1,7},{2,4},{3,5},{4,2},{5,3},{6,0},{7,1},{8,14},{9,15},{10,... | collective-permute-start | bytes 73736 | tf_op jit(solution)/shard_map/ppermute | solution.py:641
  11.7 15.6 %collective-permute-start.2 = (f32[24,256]{1,0:T(8,128)S(1)}, f32[24,256]{1,0:T(8,128)S(1)}, u32[]{:S(2)}, u32[]{:S(2)}) collective-permute-start(f32[24,256]{1,0:T(8,128)S(1)} %add.3.own_ref), channel_id=1, source_target_pairs={{0,4},{1,5},{2,6},{3,7},{4,0},{5,1},{6,2},{7,3},{8,12},{9,13},{10,... | collective-permute-start | bytes 73736 | tf_op jit(solution)/shard_map/ppermute | solution.py:641
  12.5 14.8 %collective-permute-start.1 = (f32[24,256]{1,0:T(8,128)S(1)}, f32[24,256]{1,0:T(8,128)S(1)}, u32[]{:S(2)}, u32[]{:S(2)}) collective-permute-start(f32[24,256]{1,0:T(8,128)S(1)} %add.3.own_ref), channel_id=1, source_target_pairs={{0,2},{1,3},{2,0},{3,1},{4,6},{5,7},{6,4},{7,5},{8,10},{9,11},{10,... | collective-permute-start | bytes 73736 | tf_op jit(solution)/shard_map/ppermute | solution.py:641
  13.0 14.3 %copy-start.1 = (f32[512,5,128]{2,0,1:T(8,128)S(1)}, f32[512,5,128]{2,0,1:T(8,128)}, u32[]{:S(2)}) copy-start(f32[512,5,128]{2,0,1:T(8,128)} %param.10) | copy-start | bytes 3932164
  13.0 14.3 %copy-start.6 = (f32[512,128]{1,0:T(8,128)S(1)}, f32[512,128]{1,0:T(8,128)}, u32[]{:S(2)}) copy-start(f32[512,128]{1,0:T(8,128)} %resid_ref.3) | copy-start | bytes 786436
  13.0 14.3 %copy-start.11 = (s32[512]{0:T(512)S(1)}, s32[512]{0:T(512)}, u32[]{:S(2)}) copy-start(s32[512]{0:T(512)} %param.16) | copy-start | bytes 6148
  68.8 11.3 %all-to-all-start.1 = ((f32[16,8,128]{2,1,0:T(8,128)}), f32[16,8,128]{2,1,0:T(8,128)S(1)}, u32[]{:S(2)}, u32[]{:S(2)}) async-start(f32[16,8,128]{2,1,0:T(8,128)} %solve_panels.1), calls=%async_computation.1 | async-start | bytes 131072 | tf_op jit(solution)/shard_map/all_to_all | solution.py:663

commit v2 on v1

--- a/solution.py
+++ b/solution.py
@@ -16,7 +16,8 @@
 PAIRS = [(p, q) for p in range(4) for q in range(p, 4)]
 PAIR_ROWS = 8 * len(PAIRS)
 RIGHT_ROWS = 16
-ROWS = PAIR_ROWS + RIGHT_ROWS
+BAND_ROWS = 4 * len(PAIRS)
+ROWS = 48
 STAT_ROWS = 24
 F32 = jnp.float32
 BF16 = jnp.bfloat16
@@ -63,33 +64,49 @@
 
 VMEM = pl.BlockSpec(memory_space=pltpu.VMEM)
 SMEM = pl.BlockSpec(memory_space=pltpu.SMEM)
-
-
-def stats_kernel(design_ref, weight_ref, resid_ref, source_ref, out_ref, sums_ref):
+HBM = pl.BlockSpec(memory_space=pltpu.HBM)
+
+
+def stats_kernel(
+    design_in, weight_in, resid_in, source_ref, out_ref, design_ref, weight_ref, resid_ref, sums_ref, sems
+):
+    chunks = 4
+    size = BLK_DEV // chunks
+    copies = []
+    for chunk in range(chunks):
+        at = pl.ds(chunk * size, size)
+        copies.append(
+            [
+                pltpu.make_async_copy(design_in.at[:, at], design_ref.at[:, at], sems.at[chunk, 0]),
+                pltpu.make_async_copy(weight_in.at[at], weight_ref.at[at], sems.at[chunk, 1]),
+                pltpu.make_async_copy(resid_in.at[at], resid_ref.at[at], sems.at[chunk, 2]),
+            ]
+        )
+        for copy in copies[chunk]:
+            copy.start()
     rows = 32
     lane = iota((rows, OBS), 1)
-
-    def one_group(group, carry):
-        at = pl.ds(pl.multiple_of(group * rows, rows), rows)
-        weight = weight_ref[at, :]
-        design = [design_ref[p, at, :] for p in range(5)]
-        resid = resid_ref[at, :]
-        weighted = [weight * design[p] for p in range(5)]
-        packed = jnp.zeros((rows, OBS), F32)
-        slot = 0
-        for p in range(5):
-            for q in range(p + 1):
-                total = jnp.sum(weighted[p] * design[q], axis=1, keepdims=True)
+    for chunk in range(chunks):
+        for copy in copies[chunk]:
+            copy.wait()
+        for group in range(size // rows):
+            at = pl.ds(chunk * size + group * rows, rows)
+            weight = weight_ref[at, :]
+            design = [design_ref[p, at, :] for p in range(5)]
+            resid = resid_ref[at, :]
+            weighted = [weight * design[p] for p in range(5)]
+            packed = jnp.zeros((rows, OBS), F32)
+            slot = 0
+            for p in range(5):
+                for q in range(p + 1):
+                    total = jnp.sum(weighted[p] * design[q], axis=1, keepdims=True)
+                    packed = jnp.where(lane == slot, total, packed)
+                    slot += 1
+            for p in range(5):
+                total = jnp.sum(weighted[p] * resid, axis=1, keepdims=True)
                 packed = jnp.where(lane == slot, total, packed)
                 slot += 1
-        for p in range(5):
-            total = jnp.sum(weighted[p] * resid, axis=1, keepdims=True)
-            packed = jnp.where(lane == slot, total, packed)
-            slot += 1
-        sums_ref[at, :] = packed
-        return carry
-
-    lax.fori_loop(0, BLK_DEV // rows, one_group, 0)
+            sums_ref[at, :] = packed
     local = jnp.bitwise_and(source_ref[...], SRC_DEV - 1)
     hot = (iota((SRC_DEV, BLK_DEV), 0) == local).astype(F32).astype(BF16)
     total = jnp.zeros((SRC_DEV, OBS), F32)
@@ -102,12 +119,52 @@
     return pl.pallas_call(
         stats_kernel,
         out_shape=jax.ShapeDtypeStruct((STAT_ROWS, SRC_DEV), F32),
-        in_specs=[VMEM] * 4,
+        in_specs=[HBM] * 3 + [VMEM],
         out_specs=VMEM,
-        scratch_shapes=[pltpu.VMEM((BLK_DEV, OBS), F32)],
-        compiler_params=params(16),
+        scratch_shapes=[
+            pltpu.VMEM((5, BLK_DEV, OBS), F32),
+            pltpu.VMEM((BLK_DEV, OBS), F32),
+            pltpu.VMEM((BLK_DEV, OBS), F32),
+            pltpu.VMEM((BLK_DEV, OBS), F32),
+            pltpu.SemaphoreType.DMA((4, 3)),
+        ],
+        compiler_params=params(56),
         name="source_sums",
     )(design, weight, resid, source_row)
+
+
+def roll(values, amount, axis):
+    size = values.shape[axis]
+    return pltpu.roll(values, amount % size, axis) if amount % size else values
+
+
+def convolved(first, second):
+    out = [0.0] * 7
+    for i in range(4):
+        for j in range(4):
+            out[i + j] += SPLINE[first][i] * SPLINE[second][j]
+    return out
+
+
+def fold_bands(term_ref, out_ref):
+    low_terms = [term_ref[pl.ds(k, 8, stride=8), :] for k in range(7)]
+    high_terms = [term_ref[pl.ds(64 + k, 2, stride=8), :] for k in range(7)]
+    for spacing in range(4):
+        low = high = None
+        for first in range(4 - spacing):
+            low_slot = high_slot = None
+            for k, weight in enumerate(convolved(first, first + spacing)):
+                if weight != 0.0:
+                    low_slot = plus(low_slot, weight * low_terms[k])
+                    high_slot = plus(high_slot, weight * high_terms[k])
+            low = plus(low, roll(low_slot, first, 1))
+            high = plus(high, roll(high_slot, first, 1))
+        out_ref[spacing * 10 : spacing * 10 + 8, :] = low
+        out_ref[spacing * 10 + 8 : spacing * 10 + 10, :] = high
+
+
+def plus(total, value):
+    return value if total is None else total + value
 
 
 def column_window(window_ref, block):
@@ -128,6 +185,7 @@
     poly_ref,
     pair_ref,
     total_ref,
+    joined_ref,
 ):
     named = jnp.zeros((16, BLK_DEV // 8), F32)
     capacity = list_ref.shape[1]
@@ -173,10 +231,10 @@
             pair_ref[i, at, :] = weighted[p] * comps[q]
         return carry
 
-    lax.fori_loop(0, BLK_DEV // 8, prepare, 0, unroll=2)
+    lax.fori_loop(0, BLK_DEV // 8, prepare, 0, unroll=8)
     total_ref[...] = jnp.zeros_like(total_ref)
     knot_iota = iota((KNOTS, OBS), 0)
-    unrolled = 16
+    unrolled = 64
 
     def one_group(group, carry):
         for i in range(unrolled):
@@ -199,17 +257,18 @@
 
     lax.fori_loop(0, BLK_DEV // unrolled, one_group, 0)
     for owner in range(N_SRC):
-        out_ref[owner, :PAIR_ROWS, :] = jnp.concatenate(
+        joined_ref[owner, :, :] = jnp.concatenate(
             [total_ref[2 * owner], total_ref[2 * owner + 1]], axis=1
         )
-        out_ref[owner, PAIR_ROWS:, :] = jnp.zeros((RIGHT_ROWS, OBS), F32)
+    for owner in range(N_SRC):
+        fold_bands(joined_ref.at[owner], out_ref.at[owner])
 
 
 def normal_sums(comps, phase, knots, weight, lists, counts, window):
     return pl.pallas_call(
         normals_kernel,
         out_shape=(
-            jax.ShapeDtypeStruct((N_SRC, ROWS, OBS), F32),
+            jax.ShapeDtypeStruct((N_SRC, BAND_ROWS, OBS), F32),
             jax.ShapeDtypeStruct((BLK_DEV, OBS), F32),
         ),
         in_specs=[VMEM] * 5 + [SMEM] * 2,
@@ -218,6 +277,7 @@
             pltpu.VMEM((BLK_DEV * 8, OBS), F32),
             pltpu.VMEM((len(PAIRS), BLK_DEV, OBS), F32),
             pltpu.VMEM((N_COL, PAIR_ROWS, KNOTS), F32),
+            pltpu.VMEM((N_SRC, PAIR_ROWS, OBS), F32),
         ],
         compiler_params=params(32),
         cost_estimate=pl.CostEstimate(flops=3_000_000_000, bytes_accessed=4_000_000, transcendentals=0),
@@ -271,15 +331,13 @@
     knot_ref,
     source_ref,
     window_ref,
-    sums_in_ref,
+    bands_ref,
     step_ref,
     first_ref,
     sums_ref,
     column_ref,
     term_ref,
     total_ref,
-    right_ref,
-    sem,
 ):
     totals = (own_ref[...] + near_ref[...]) + (far_ref[...] + cross_ref[...])
     step = solve_five(totals)
@@ -310,10 +368,10 @@
                 term_ref[pl.ds(group * 128 + 4 * m + p, 8, stride=16), :] = scaled * comps[p]
         return carry
 
-    lax.fori_loop(0, BLK_DEV // 8, prepare, 0, unroll=2)
+    lax.fori_loop(0, BLK_DEV // 8, prepare, 0, unroll=8)
     total_ref[...] = jnp.zeros_like(total_ref)
     knot_iota = iota((KNOTS, OBS), 0)
-    unrolled = 16
+    unrolled = 64
 
     def one_group(group, carry):
         for i in range(unrolled):
@@ -333,10 +391,12 @@
 
     lax.fori_loop(0, BLK_DEV // unrolled, one_group, 0)
     for owner in range(N_SRC):
-        right_ref[owner] = jnp.concatenate([total_ref[2 * owner], total_ref[2 * owner + 1]], axis=1)
-    copy = pltpu.make_async_copy(right_ref, sums_ref.at[:, PAIR_ROWS:ROWS, :], sem)
-    copy.start()
-    copy.wait()
+        joined = jnp.concatenate([total_ref[2 * owner], total_ref[2 * owner + 1]], axis=1)
+        right = joined[:4]
+        for first in range(1, 4):
+            right = right + roll(joined[4 * first : 4 * first + 4], first, 1)
+        sums_ref[owner, :BAND_ROWS, :] = bands_ref[owner]
+        sums_ref[owner, BAND_ROWS:, :] = jnp.concatenate([right, jnp.zeros((4, OBS), F32)], axis=0)
 
 
 def right_sums(parts, design, resid, watt, comps, phase, knots, source_row, window, sums):
@@ -347,68 +407,35 @@
             jax.ShapeDtypeStruct((BLK_DEV, OBS), F32),
             jax.ShapeDtypeStruct((N_SRC, ROWS, OBS), F32),
         ),
-        in_specs=[VMEM] * 11 + [SMEM, pl.BlockSpec(memory_space=pl.ANY)],
-        out_specs=(VMEM, VMEM, pl.BlockSpec(memory_space=pl.ANY)),
+        in_specs=[VMEM] * 11 + [SMEM, VMEM],
+        out_specs=(VMEM, VMEM, VMEM),
         scratch_shapes=[
             pltpu.VMEM((BLK_DEV, OBS), F32),
             pltpu.VMEM((BLK_DEV * 16, OBS), F32),
             pltpu.VMEM((N_COL, RIGHT_ROWS, KNOTS), F32),
-            pltpu.VMEM((N_SRC, RIGHT_ROWS, OBS), F32),
-            pltpu.SemaphoreType.DMA,
         ],
-        input_output_aliases={12: 2},
         compiler_params=params(32),
         name="right_sums",
     )(*parts, design, resid, watt, comps, phase, knots, source_row, window, sums)
 
 
-def roll(values, amount, axis):
-    size = values.shape[axis]
-    return pltpu.roll(values, amount % size, axis) if amount % size else values
-
-
-def convolved(first, second):
-    out = [0.0] * 7
-    for i in range(4):
-        for j in range(4):
-            out[i + j] += SPLINE[first][i] * SPLINE[second][j]
-    return out
-
-
-def solve_kernel(prior, got_ref, out_ref, sum_ref, work_ref):
+def solve_kernel(prior, got_ref, out_ref, work_ref):
     total = got_ref[0]
     for other in range(1, N_SRC):
         total = total + got_ref[other]
-    sum_ref[...] = total
     lane8 = iota((8, OBS), 1)
     sublane8 = iota((8, OBS), 0)
-    low_terms = [sum_ref[pl.ds(k, 8, stride=8), :] for k in range(7)]
-    high_terms = [sum_ref[pl.ds(64 + k, 2, stride=8), :] for k in range(7)]
+    index = {}
+    for i, (p, q) in enumerate(PAIRS):
+        index[p, q] = index[q, p] = i
     bands = []
     for spacing in range(4):
-        low = jnp.zeros((8, OBS), F32)
-        high = jnp.zeros((2, OBS), F32)
-        for first in range(4 - spacing):
-            weights = convolved(first, first + spacing)
-            low_slot = jnp.zeros((8, OBS), F32)
-            high_slot = jnp.zeros((2, OBS), F32)
-            for k in range(7):
-                if weights[k] != 0.0:
-                    low_slot = low_slot + weights[k] * low_terms[k]
-                    high_slot = high_slot + weights[k] * high_terms[k]
-            low = low + roll(low_slot, first, 1)
-            high = high + roll(high_slot, first, 1)
-        rows = [low[i : i + 1] for i in range(8)] + [high[i : i + 1] for i in range(2)]
+        rows = [total[spacing * 10 + i : spacing * 10 + i + 1] for i in range(10)]
         if spacing == 0:
             rows = [row + prior if PAIRS[i][0] == PAIRS[i][1] else row for i, row in enumerate(rows)]
-        index = {}
-        for i, (p, q) in enumerate(PAIRS):
-            index[p, q] = index[q, p] = i
         full = [rows[index[p, q]] for p in range(4) for q in range(4)]
         bands.append([jnp.concatenate(full[:8], axis=0), jnp.concatenate(full[8:], axis=0)])
-    right = sum_ref[PAIR_ROWS : PAIR_ROWS + 4, :]
-    for first in range(1, 4):
-        right = right + roll(sum_ref[PAIR_ROWS + 4 * first : PAIR_ROWS + 4 * first + 4, :], first, 1)
+    right = total[BAND_ROWS : BAND_ROWS + 4]
     right = jnp.concatenate([right, right], axis=0)
 
     place = jnp.bitwise_and(lane8, 31)
@@ -424,12 +451,13 @@
         down = jnp.where(step - spacing >= HALF, 0.0, down)
         return jnp.where(is_down, down, up)
 
-    stream = [arranged(bands[d][h], d, 0) for d in range(4) for h in range(2)] + [
-        arranged(right, 0, 0)
-    ]
-    tail = [arranged(bands[d][h], d, 32) for d in range(4) for h in range(2)] + [
-        arranged(right, 0, 32)
-    ]
+    def entering(base):
+        return [arranged(bands[d][h], d, base) for d in range(4) for h in range(2)] + [
+            arranged(right, 0, base)
+        ]
+
+    stream, tail = entering(0), entering(32)
+
     lower = sublane8 < 4
 
     def insert(front, target, pieces, slot, present):
@@ -457,50 +485,42 @@
         target[slot // 2] = jnp.where(keep, target[slot // 2], pieces[8])
 
     def eliminate(front, target, slot, gone):
+        scale = None
         for p in range(4):
             row = slot * 4 + p
             half, at = row // 8, row % 8
             column = front[row]
             inverse = 1.0 / column[half][at : at + 1, :]
+            scale = inverse if scale is None else jnp.where(sublane8 == at, inverse, scale)
+            factor = [column[h] * inverse for h in range(2)]
+            factor[half] = jnp.where(sublane8 == at, 0.0, factor[half])
             gone = gone | {row}
             for c in [c for c in range(16) if c not in gone] + [16]:
                 values = target if c == 16 else front[c]
-                factor = values[half][at : at + 1, :] * inverse
+                pivot = values[half][at : at + 1, :]
                 for h in range(2):
-                    values[h] = values[h] - column[h] * factor
-                values[half] = jnp.where(sublane8 == at, factor, values[half])
-        return gone
-
-    def save(front, target, slot, step):
+                    values[h] = values[h] - factor[h] * pivot
+        return gone, scale
+
+    def save(front, target, slot, step, scale):
         for r in range(1, 4):
             for q in range(4):
-                work_ref[step * 13 + (r - 1) * 4 + q] = front[(slot + r) % 4 * 4 + q][slot // 2]
-        work_ref[step * 13 + 12] = target[slot // 2]
+                work_ref[step * 13 + (r - 1) * 4 + q] = (
+                    front[(slot + r) % 4 * 4 + q][slot // 2] * scale
+                )
+        work_ref[step * 13 + 12] = target[slot // 2] * scale
 
     zero = jnp.zeros((8, OBS), F32)
     front = [[zero, zero] for _ in range(16)]
     target = [zero, zero]
     for step in range(4):
-        insert(front, target, stream, step, step)
-        stream = [roll(values, -1, 1) for values in stream]
-
-    def four_knots(turn, carry):
-        front = [list(pair) for pair in carry[0]]
-        target = list(carry[1])
-        stream = list(carry[2])
-        for slot in range(4):
-            eliminate(front, target, slot, frozenset())
-            save(front, target, slot, turn * 4 + slot)
-            insert(front, target, stream, slot, 3)
-            stream = [roll(values, -1, 1) for values in stream]
-        return (front, target, stream)
-
-    front, target, stream = lax.fori_loop(0, 7, four_knots, (front, target, stream))
-    for slot in range(2):
-        eliminate(front, target, slot, frozenset())
-        save(front, target, slot, 28 + slot)
-        insert(front, target, tail, slot, 3)
-        tail = [roll(values, -1, 1) for values in tail]
+        insert(front, target, [roll(values, -step, 1) for values in stream], step, step)
+    for step in range(HALF):
+        slot = step % 4
+        unused, scale = eliminate(front, target, slot, frozenset())
+        save(front, target, slot, step, scale)
+        source, shift = (stream, step + 4) if step < 28 else (tail, step - 28)
+        insert(front, target, [roll(values, -shift, 1) for values in source], slot, 3)
 
     mirror = jnp.bitwise_xor(lane8, 32)
 
@@ -514,46 +534,46 @@
     ]
     target = [target[h] + mirrored(target[1 - h]) for h in range(2)]
     gone = frozenset()
+    scales = {}
     for slot in (2, 3, 0, 1):
-        gone = eliminate(front, target, slot, gone)
+        gone, scales[slot] = eliminate(front, target, slot, gone)
+    target = [
+        target[h] * jnp.where(lower, scales[2 * h], scales[2 * h + 1]) for h in range(2)
+    ]
 
     first_lane = place == 0
-
-    def emit(result, answer, slot):
+    placed = []
+
+    def emit(answer, slot, step):
         values = answer[slot // 2]
         values = values if slot % 2 == 0 else roll(values, 4, 0)
-        return jnp.where(first_lane, values, roll(result, 1, 1))
+        placed.append(roll(jnp.where(first_lane, values, 0.0), step, 1))
 
     def back(answer, slot, step):
         half = slot // 2
-        sums = [work_ref[step * 13 + 12], zero]
+        parts = [work_ref[step * 13 + 12]]
         for r in (3, 2, 1):
             other = (slot + r) % 4
+            terms = []
             for q in range(4):
                 at = other % 2 * 4 + q
-                sums[q % 2] = sums[q % 2] - work_ref[step * 13 + (r - 1) * 4 + q] * (
-                    answer[other // 2][at : at + 1, :]
+                terms.append(
+                    work_ref[step * 13 + (r - 1) * 4 + q] * answer[other // 2][at : at + 1, :]
                 )
-        fresh = sums[0] + sums[1]
+            parts.append((terms[0] + terms[1]) + (terms[2] + terms[3]))
+        fresh = ((parts[0] - parts[1]) - parts[2]) - parts[3]
         keep = lower if slot % 2 == 1 else jnp.logical_not(lower)
         answer[half] = jnp.where(keep, answer[half], fresh)
 
     answer = list(target)
-    result = emit(zero, answer, 3)
-    result = emit(result, answer, 2)
-    for slot in (1, 0):
-        back(answer, slot, 28 + slot)
-        result = emit(result, answer, slot)
-
-    def four_back(turn, carry):
-        answer = list(carry[0])
-        result = carry[1]
-        for slot in (3, 2, 1, 0):
-            back(answer, slot, (6 - turn) * 4 + slot)
-            result = emit(result, answer, slot)
-        return (answer, result)
-
-    answer, result = lax.fori_loop(0, 7, four_back, (answer, result))
+    emit(answer, 3, 31)
+    emit(answer, 2, 30)
+    for step in range(HALF - 1, -1, -1):
+        back(answer, step % 4, step)
+        emit(answer, step % 4, step)
+    while len(placed) > 1:
+        placed = [placed[i] + placed[i + 1] for i in range(0, len(placed), 2)]
+    result = placed[0]
     knot = jnp.bitwise_and(lane8, KNOTS - 1)
     from_lane = jnp.where(knot < 32, lane8, window_at + 32 + KNOTS - 1 - knot)
     panel = jnp.take_along_axis(result, from_lane, axis=1)
@@ -570,10 +590,7 @@
         out_shape=jax.ShapeDtypeStruct((N_SRC, 8, OBS), F32),
         in_specs=[VMEM],
         out_specs=VMEM,
-        scratch_shapes=[
-            pltpu.VMEM((ROWS, OBS), F32),
-            pltpu.VMEM((HALF * 13, 8, OBS), F32),
-        ],
+        scratch_shapes=[pltpu.VMEM((HALF * 13, 8, OBS), F32)],
         compiler_params=params(16),
         name="solve_panels",
     )(got)
@@ -602,7 +619,7 @@
         out_ref[at, :] = first_ref[at, :] - total
         return carry
 
-    lax.fori_loop(0, BLK_DEV // 8, one_group, 0, unroll=4)
+    lax.fori_loop(0, BLK_DEV // 8, one_group, 0, unroll=16)
 
 
 def final_residual(panels, comps, phase, knots, first, window):

time: 85.9 us -> 66.3 us (0.77)
  Pallas kernels: 42.6 us -> 30.1 us
  blocking collectives: 21.5 us -> 17.2 us
  local copies, waits for them, and re-layouts: 5.44 us -> 1.54 us
    pallas_call x1, Pallas kernels: 14.3 us -> 9.04 us  [normal_sums(): pl.pallas_call(normals_kernel, out_shape=(jax.ShapeDtypeStruct((N_SRC, BA...]
    pallas_call x1, Pallas kernels: 13.8 us -> 8.88 us  [right_sums(): pl.pallas_call(rights_kernel, out_shape=(jax.ShapeDtypeStruct((5, SRC_DEV...]
    all_to_all x1, blocking collectives: 21.5 us -> 17.2 us  [shards(): got = lax.all_to_all(sums, 'src', split_axis=0, concat_axis=0, tiled=True)]
    unnamed x28 -> x20, local copies, waits for them, and re-layouts: 3.95 us -> 0.05 us
    pallas_call x1, Pallas kernels: 6.03 us -> 3.11 us  [solve_panels(): pl.pallas_call(body, out_shape=jax.ShapeDtypeStruct((N_SRC, 8, OBS), F32)...]
    pallas_call x1, Pallas kernels: 3.02 us -> 4.54 us  [source_sums(): pl.pallas_call(stats_kernel, out_shape=jax.ShapeDtypeStruct((STAT_ROWS, S...]
    pallas_call x1, Pallas kernels: 5.45 us -> 4.54 us  [final_residual(): pl.pallas_call(final_kernel, out_shape=jax.ShapeDtypeStruct((BLK_DEV, OBS...]
  transfers between devices with their start and end apart: 5 -> 5, of which waited for: 2 -> 2; matrix products, arithmetic and copies ran while one was open for 2% -> 2% of each run, Pallas kernels for 17% -> 14%
where the time goes in v2:
time: 66.3 us; the launch traced here: 65.9 us
  Pallas kernels  30.1 us (45%)
  blocking collectives  17.2 us (26%)
  starting transfers between devices  7.89 us (12%)
  waiting for transfers between devices  7.57 us (11%)
  local copies, waits for them, and re-layouts  1.54 us (2%)
  between operations  0.83 us (1%)
  other arithmetic  0.74 us (1%)
    all_to_all x1, blocking collectives, shards(): got = lax.all_to_all(sums, 'src', split_axis=0, concat_axis=0, tiled=True)  17.2 us
    pallas_call x1, Pallas kernels, normal_sums(): pl.pallas_call(normals_kernel, out_shape=(jax.ShapeDtypeStruct((N_SRC, BA...  9.04 us
    pallas_call x1, Pallas kernels, right_sums(): pl.pallas_call(rights_kernel, out_shape=(jax.ShapeDtypeStruct((5, SRC_DEV...  8.88 us
    all_to_all x1, waiting for transfers between devices, shards(): lax.all_to_all(own_panels, 'src', split_axis=0, concat_axis=0, tiled=True)  6.17 us
    pallas_call x1, Pallas kernels, final_residual(): pl.pallas_call(final_kernel, out_shape=jax.ShapeDtypeStruct((BLK_DEV, OBS...  4.54 us
    pallas_call x1, Pallas kernels, source_sums(): pl.pallas_call(stats_kernel, out_shape=jax.ShapeDtypeStruct((STAT_ROWS, S...  4.54 us
    ppermute x4, starting transfers between devices, swap(): return lax.ppermute(values, 'win', [(i, i ^ bit) for i in range(n_win)])  4.18 us
    all_to_all x1, starting transfers between devices, shards(): lax.all_to_all(own_panels, 'src', split_axis=0, concat_axis=0, tiled=True)  3.71 us
  transfers between devices with their start and end apart: 5, of which 2 were waited for; matrix products, arithmetic and copies ran while one was open for 2% of the time, Pallas kernels for 14%

profile of v2, /device:TPU:0, one launch (start us, length us, event | category | flops | bytes accessed | tf_op | source)
XLA Modules:
  0.0 65.9 jit_solution(4542809267369482372)
XLA Ops:
  0.7 4.5 %source_sums.1 = f32[24,256]{1,0:T(8,128)} custom-call(f32[5,512,128]{2,1,0:T(8,128)} %bitcast.6, f32[512,128]{1,0:T(8,128)} %weight_ref.1, f32[512,128]{1,0:T(8,128)} %resid_ref.1, s32[1,512]{1,0:T(1,128)} %bitcast.11), custom_call_target="tpu_custom_call" | custom-call | tf_op jit(solution)/shard_map/source_sums/pallas_call | solution.py:119
  5.2 0.1 collective-permute-start
  5.3 1.4 %collective-permute-done = f32[24,256]{1,0:T(8,128)S(1)} collective-permute-done((f32[24,256]{1,0:T(8,128)}, f32[24,256]{1,0:T(8,128)S(1)}, u32[]{:S(2)}, u32[]{:S(2)}) %collective-permute-start) | collective-permute-done | bytes 24608 | tf_op jit(solution)/shard_map/ppermute | solution.py:658
  6.7 0.7 %add.3.own_ref = f32[24,256]{1,0:T(8,128)S(1)} add(f32[24,256]{1,0:T(8,128)} %source_sums.1, f32[24,256]{1,0:T(8,128)S(1)} %collective-permute-done) | non-fusion elementwise | flops 6144 | bytes 73728 | tf_op jit(solution)/shard_map/add | solution.py:661
  7.5 2.8 %collective-permute-start.3 = (f32[24,256]{1,0:T(8,128)S(1)}, f32[24,256]{1,0:T(8,128)S(1)}, u32[]{:S(2)}, u32[]{:S(2)}) collective-permute-start(f32[24,256]{1,0:T(8,128)S(1)} %add.3.own_ref), channel_id=1, source_target_pairs={{0,6},{1,7},{2,4},{3,5},{4,2},{5,3},{6,0},{7,1},{8,14},{9,15},{10,... | collective-permute-start | bytes 73736 | tf_op jit(solution)/shard_map/ppermute | solution.py:658
  10.3 0.8 %collective-permute-start.2 = (f32[24,256]{1,0:T(8,128)S(1)}, f32[24,256]{1,0:T(8,128)S(1)}, u32[]{:S(2)}, u32[]{:S(2)}) collective-permute-start(f32[24,256]{1,0:T(8,128)S(1)} %add.3.own_ref), channel_id=1, source_target_pairs={{0,4},{1,5},{2,6},{3,7},{4,0},{5,1},{6,2},{7,3},{8,12},{9,13},{10,... | collective-permute-start | bytes 73736 | tf_op jit(solution)/shard_map/ppermute | solution.py:658
  11.1 0.5 collective-permute-start.1
  11.6 0.0 copy-done.6
  11.6 0.0 copy-start
  11.6 0.0 copy-start.4
  11.6 0.0 copy-start.7
  11.7 9.0 %normal_sums.1 = (f32[16,40,128]{2,1,0:T(8,128)S(1)}, f32[512,128]{1,0:T(8,128)S(1)}) custom-call(f32[2048,128]{1,0:T(8,128)S(1)} %bitcast.8, f32[512,128]{1,0:T(8,128)S(1)} %copy-done.2, s32[512,128]{1,0:T(8,128)S(1)} %copy-done.3, f32[512,128]{1,0:T(8,128)S(1)} %copy-done.5, s32[16,64]{1,0:T(8,128)S(1)} %copy-done.8, s32[16]{0:T(128)S(1)} %copy-done.9, ...), custom_call_target="tpu_custom_call" | custom-call | flops 3000000000 | bytes 4000000 | tf_op jit(solution)/shard_map/normal_sums/pallas_call | solution.py:268
  20.7 0.0 collective-permute-done.3.cross_ref
  20.7 0.0 collective-permute-done.2.far_ref
  20.7 0.0 collective-permute-done.1.near_ref
  20.8 8.9 %right_sums.1 = (f32[5,256]{1,0:T(8,128)}, f32[512,128]{1,0:T(8,128)S(1)}, f32[16,48,128]{2,1,0:T(8,128)S(1)}) custom-call(f32[24,256]{1,0:T(8,128)S(1)} %add.3.own_ref, f32[24,256]{1,0:T(8,128)S(1)} %collective-permute-done.1.near_ref, f32[24,256]{1,0:T(8,128)S(1)} %collective-permute-done.2.far_ref, f32[24,256]{1,0:T(8,128)S(1)} %collective-permute-done.3.cross_ref, ...), custom_call_target="tpu_custom_call" | custom-call | tf_op jit(solution)/shard_map/right_sums/pallas_call | solution.py:403
  29.6 17.2 %all_to_all.10.refs_0_ = f32[16,48,128]{2,1,0:T(8,128)S(1)} all-to-all(f32[16,48,128]{2,1,0:T(8,128)S(1)} %get-tuple-element.11), channel_id=1, replica_groups=mesh['src'=16,'win'=8] {'src'}, dimensions={0} | all-to-all | bytes 786432 | tf_op jit(solution)/shard_map/all_to_all | solution.py:678
  46.9 3.1 %solve_panels.1 = f32[16,8,128]{2,1,0:T(8,128)} custom-call(f32[16,48,128]{2,1,0:T(8,128)S(1)} %all_to_all.10.refs_0_), custom_call_target="tpu_custom_call" | custom-call | tf_op jit(solution)/shard_map/solve_panels/pallas_call | solution.py:588
  50.0 3.7 %all-to-all-start.1 = ((f32[16,8,128]{2,1,0:T(8,128)}), f32[16,8,128]{2,1,0:T(8,128)S(1)}, u32[]{:S(2)}, u32[]{:S(2)}) async-start(f32[16,8,128]{2,1,0:T(8,128)} %solve_panels.1), calls=%async_computation.1 | async-start | bytes 131072 | tf_op jit(solution)/shard_map/all_to_all | solution.py:680
  53.7 0.7 %slice.4 = f32[1,4,128]{2,1,0:T(4,128)S(1)} slice(f32[16,8,128]{2,1,0:T(8,128)} %solve_panels.1), slice={[0:1], [0:4], [0:128]} | slice | bytes 4096 | tf_op jit(solution)/shard_map/slice | solution.py:682
  54.4 0.1 copy.15
  54.5 0.7 %reshape.17 = f32[2,256]{1,0:T(2,128)} reshape(f32[2,64,4]{2,1,0:T(8,128)S(1)} %bitcast.13) | data formatting | bytes 4096 | tf_op jit(solution)/shard_map/reshape | solution.py:682
  55.2 6.2 %all-to-all-done.1.panel_ref = f32[16,8,128]{2,1,0:T(8,128)S(1)} async-done(((f32[16,8,128]{2,1,0:T(8,128)}), f32[16,8,128]{2,1,0:T(8,128)S(1)}, u32[]{:S(2)}, u32[]{:S(2)}) %all-to-all-start.1) | async-done | bytes 65568 | tf_op jit(solution)/shard_map/all_to_all | solution.py:680
  61.4 4.5 %final_residual.1 = f32[512,128]{1,0:T(8,128)} custom-call(f32[16,8,128]{2,1,0:T(8,128)S(1)} %all-to-all-done.1.panel_ref, f32[2048,128]{1,0:T(8,128)S(1)} %bitcast.10, f32[512,128]{1,0:T(8,128)S(1)} %copy-done.2, s32[512,128]{1,0:T(8,128)S(1)} %copy-done.3, f32[512,128]{1,0:T(8,128)S(1)} %get-tuple-element.12.first_ref, s32[512]{0:T(512)S(1)} %copy-done.6), custom_call_target="tpu_custom_call" | custom-call | tf_op jit(solution)/shard_map/final_residual/pallas_call | solution.py:626
  (16 shorter events, 0.0 us)
Async XLA Ops:
  0.6 10.9 %copy-start.5 = (f32[512,128]{1,0:T(8,128)S(1)}, f32[512,128]{1,0:T(8,128)}, u32[]{:S(2)}) copy-start(f32[512,128]{1,0:T(8,128)} %weight_ref.1) | copy-start | bytes 786436
  0.6 10.9 %copy-start.6 = (s32[512]{0:T(512)S(1)}, s32[512]{0:T(512)}, u32[]{:S(2)}) copy-start(s32[512]{0:T(512)} %window_ref.5) | copy-start | bytes 6148
  0.7 10.9 %copy-start.3 = (s32[512,128]{1,0:T(8,128)S(1)}, s32[512,128]{1,0:T(8,128)}, u32[]{:S(2)}) copy-start(s32[512,128]{1,0:T(8,128)} %knot_ref.5) | copy-start | bytes 786436
  0.7 10.9 %copy-start.2 = (f32[512,128]{1,0:T(8,128)S(1)}, f32[512,128]{1,0:T(8,128)}, u32[]{:S(2)}) copy-start(f32[512,128]{1,0:T(8,128)} %phase_ref.5) | copy-start | bytes 786436
  0.7 10.9 %copy-start.9 = (s32[16]{0:T(128)S(1)}, s32[16]{0:T(128)}, u32[]{:S(2)}) copy-start(s32[16]{0:T(128)} %count_ref.1) | copy-start | bytes 196
  0.7 10.9 %copy-start.8 = (s32[16,64]{1,0:T(8,128)S(1)}, s32[16,64]{1,0:T(8,128)}, u32[]{:S(2)}) copy-start(s32[16,64]{1,0:T(8,128)} %list_ref.1) | copy-start | bytes 12292
  0.7 10.9 %copy-start.1 = (f32[512,4,128]{2,1,0:T(4,128)S(1)}, f32[512,4,128]{2,1,0:T(4,128)}, u32[]{:S(2)}) copy-start(f32[512,4,128]{2,1,0:T(4,128)} %param.11) | copy-start | bytes 3145732
  5.2 1.5 %collective-permute-start = (f32[24,256]{1,0:T(8,128)}, f32[24,256]{1,0:T(8,128)S(1)}, u32[]{:S(2)}, u32[]{:S(2)}) collective-permute-start(f32[24,256]{1,0:T(8,128)} %source_sums.1), channel_id=1, source_target_pairs={{0,1},{1,0},{2,3},{3,2},{4,5},{5,4},{6,7},{7,6},{8,9},{9,8},{10,11... | collective-permute-start | bytes 73736 | tf_op jit(solution)/shard_map/ppermute | solution.py:658
  7.5 13.2 %collective-permute-start.3 = (f32[24,256]{1,0:T(8,128)S(1)}, f32[24,256]{1,0:T(8,128)S(1)}, u32[]{:S(2)}, u32[]{:S(2)}) collective-permute-start(f32[24,256]{1,0:T(8,128)S(1)} %add.3.own_ref), channel_id=1, source_target_pairs={{0,6},{1,7},{2,4},{3,5},{4,2},{5,3},{6,0},{7,1},{8,14},{9,15},{10,... | collective-permute-start | bytes 73736 | tf_op jit(solution)/shard_map/ppermute | solution.py:658
  10.3 10.4 %collective-permute-start.2 = (f32[24,256]{1,0:T(8,128)S(1)}, f32[24,256]{1,0:T(8,128)S(1)}, u32[]{:S(2)}, u32[]{:S(2)}) collective-permute-start(f32[24,256]{1,0:T(8,128)S(1)} %add.3.own_ref), channel_id=1, source_target_pairs={{0,4},{1,5},{2,6},{3,7},{4,0},{5,1},{6,2},{7,3},{8,12},{9,13},{10,... | collective-permute-start | bytes 73736 | tf_op jit(solution)/shard_map/ppermute | solution.py:658
  11.1 9.6 %collective-permute-start.1 = (f32[24,256]{1,0:T(8,128)S(1)}, f32[24,256]{1,0:T(8,128)S(1)}, u32[]{:S(2)}, u32[]{:S(2)}) collective-permute-start(f32[24,256]{1,0:T(8,128)S(1)} %add.3.own_ref), channel_id=1, source_target_pairs={{0,2},{1,3},{2,0},{3,1},{4,6},{5,7},{6,4},{7,5},{8,10},{9,11},{10,... | collective-permute-start | bytes 73736 | tf_op jit(solution)/shard_map/ppermute | solution.py:658
  11.6 9.1 %copy-start = (f32[512,5,128]{2,0,1:T(8,128)S(1)}, f32[512,5,128]{2,0,1:T(8,128)}, u32[]{:S(2)}) copy-start(f32[512,5,128]{2,0,1:T(8,128)} %param.10) | copy-start | bytes 3932164
  11.6 9.1 %copy-start.4 = (f32[512,128]{1,0:T(8,128)S(1)}, f32[512,128]{1,0:T(8,128)}, u32[]{:S(2)}) copy-start(f32[512,128]{1,0:T(8,128)} %resid_ref.1) | copy-start | bytes 786436
  11.6 9.1 %copy-start.7 = (s32[512]{0:T(512)S(1)}, s32[512]{0:T(512)}, u32[]{:S(2)}) copy-start(s32[512]{0:T(512)} %param.16) | copy-start | bytes 6148
  50.0 11.4 %all-to-all-start.1 = ((f32[16,8,128]{2,1,0:T(8,128)}), f32[16,8,128]{2,1,0:T(8,128)S(1)}, u32[]{:S(2)}, u32[]{:S(2)}) async-start(f32[16,8,128]{2,1,0:T(8,128)} %solve_panels.1), calls=%async_computation.1 | async-start | bytes 131072 | tf_op jit(solution)/shard_map/all_to_all | solution.py:680

commit v3 on v2

--- a/solution.py
+++ b/solution.py
@@ -19,6 +19,9 @@
 BAND_ROWS = 4 * len(PAIRS)
 ROWS = 48
 STAT_ROWS = 24
+CODES = 384
+N_PAIR = 272
+NO_BLOCK = 512
 F32 = jnp.float32
 BF16 = jnp.bfloat16
 NT = (((1,), (1,)), ((), ()))
@@ -59,12 +62,17 @@
 
 
 def params(megabytes):
-    return pltpu.CompilerParams(vmem_limit_bytes=megabytes * 1024 * 1024)
+    return pltpu.CompilerParams(vmem_limit_bytes=int(megabytes * 1024 * 1024))
 
 
 VMEM = pl.BlockSpec(memory_space=pltpu.VMEM)
 SMEM = pl.BlockSpec(memory_space=pltpu.SMEM)
 HBM = pl.BlockSpec(memory_space=pltpu.HBM)
+
+
+def column_window(window_ref, block):
+    window = window_ref[block]
+    return lax.shift_right_logical(window, 4) * 2 + jnp.bitwise_and(window, 1)
 
 
 def stats_kernel(
@@ -118,7 +126,7 @@
 def source_sums(design, weight, resid, source_row):
     return pl.pallas_call(
         stats_kernel,
-        out_shape=jax.ShapeDtypeStruct((STAT_ROWS, SRC_DEV), F32),
+        out_shape=pltpu.VMEM((STAT_ROWS, SRC_DEV), F32),
         in_specs=[HBM] * 3 + [VMEM],
         out_specs=VMEM,
         scratch_shapes=[
@@ -128,9 +136,9 @@
             pltpu.VMEM((BLK_DEV, OBS), F32),
             pltpu.SemaphoreType.DMA((4, 3)),
         ],
-        compiler_params=params(56),
+        compiler_params=params(54),
         name="source_sums",
-    )(design, weight, resid, source_row)
+    )(*(pltpu.with_memory_space_constraint(x, pltpu.HBM) for x in (design, weight, resid)), source_row)
 
 
 def roll(values, amount, axis):
@@ -167,9 +175,50 @@
     return value if total is None else total + value
 
 
-def column_window(window_ref, block):
-    window = window_ref[block]
-    return lax.shift_right_logical(window, 4) * 2 + jnp.bitwise_and(window, 1)
+def pair_members(code_ref, pair):
+    code = code_ref[0, pair]
+    blocks = []
+    for shift in (0, 10):
+        block = jnp.bitwise_and(lax.shift_right_logical(code, shift), 1023)
+        blocks.append((jnp.minimum(block, BLK_DEV - 1), jnp.bitwise_and(block, NO_BLOCK)))
+    return lax.shift_right_logical(code, 20), blocks
+
+
+def pair_codes(window):
+    column = lax.shift_right_logical(window, 4) * 2 + jnp.bitwise_and(window, 1)
+    hot = (iota((N_COL, BLK_DEV), 0) == column).astype(F32)
+    before = (iota((OBS, OBS), 0) < iota((OBS, OBS), 1)).astype(F32).astype(BF16)
+    count = jnp.zeros((N_COL, 1), F32)
+    ranks = []
+    for start in range(0, BLK_DEV, OBS):
+        part = hot[:, start : start + OBS]
+        seen = jnp.dot(part.astype(BF16), before, preferred_element_type=F32) + count
+        ranks.append(jnp.sum(part * seen, axis=0, keepdims=True))
+        count = count + jnp.sum(part, axis=1, keepdims=True)
+    rank = jnp.concatenate(ranks, axis=1).astype(jnp.int32)
+    pairs = lax.shift_right_logical(count.astype(jnp.int32) + 1, 1).astype(F32)
+    below = (iota((N_COL, N_COL), 1) < iota((N_COL, N_COL), 0)).astype(F32).astype(BF16)
+    spread = jnp.broadcast_to(pairs, (N_COL, OBS)).astype(BF16)
+    start = jnp.dot(below, spread, preferred_element_type=F32)[:, :1]
+    pair = jnp.sum(hot * start, axis=0, keepdims=True).astype(jnp.int32)
+    pair = pair + lax.shift_right_logical(rank, 1)
+    second = jnp.bitwise_and(rank, 1)
+    missing = NO_BLOCK - iota((1, BLK_DEV), 1)
+    high, low = lax.shift_right_logical(missing, 4), jnp.bitwise_and(missing, 15)
+    first = 1 - second
+    rows = [first * high, first * low, second * high, second * low, first * column]
+    rows = jnp.concatenate([row.astype(F32) for row in rows] + [jnp.zeros((11, BLK_DEV), F32)], axis=0)
+    target = (iota((CODES, BLK_DEV), 0) == pair).astype(F32).astype(BF16)
+    found = lax.dot_general(rows.astype(BF16), target, NT, preferred_element_type=F32)
+    found = found.astype(jnp.int32)
+    left = NO_BLOCK - found[0:1] * 16 - found[1:2]
+    right = NO_BLOCK - found[2:3] * 16 - found[3:4]
+    return left + right * 1024 + found[4:5] * (1 << 20)
+
+
+def knots_hot(knot_ref, block, offset):
+    hot = iota((KNOTS, OBS), 0) == knot_ref[pl.ds(block, 1), :] + offset
+    return hot.astype(F32).astype(BF16)
 
 
 def normals_kernel(
@@ -178,15 +227,18 @@
     knot_ref,
     weight_ref,
     list_ref,
+    window_row_ref,
     count_ref,
     window_ref,
     out_ref,
     watt_ref,
+    code_ref,
     poly_ref,
     pair_ref,
     total_ref,
     joined_ref,
 ):
+    code_ref[...] = pair_codes(window_row_ref[...])
     named = jnp.zeros((16, BLK_DEV // 8), F32)
     capacity = list_ref.shape[1]
     slot = iota((1, capacity), 1)
@@ -231,10 +283,9 @@
             pair_ref[i, at, :] = weighted[p] * comps[q]
         return carry
 
-    lax.fori_loop(0, BLK_DEV // 8, prepare, 0, unroll=8)
+    lax.fori_loop(0, BLK_DEV // 8, prepare, 0, unroll=16)
     total_ref[...] = jnp.zeros_like(total_ref)
-    knot_iota = iota((KNOTS, OBS), 0)
-    unrolled = 64
+    unrolled = 128
 
     def one_group(group, carry):
         for i in range(unrolled):
@@ -243,16 +294,15 @@
             terms = jnp.concatenate(
                 [poly * pair_ref[n, pl.ds(block, 1), :] for n in range(len(PAIRS))], axis=0
             )
-            high, low = split2(terms)
-            hot = (knot_iota == knot_ref[pl.ds(block, 1), :]).astype(F32).astype(BF16)
+            hot = knots_hot(knot_ref, block, 0)
             summed = lax.dot_general(
-                jnp.concatenate([high, low], axis=1),
+                jnp.concatenate(split2(terms), axis=1),
                 jnp.concatenate([hot, hot], axis=1),
                 NT,
                 preferred_element_type=F32,
             )
-            at = column_window(window_ref, block)
-            total_ref[at] = total_ref[at] + summed
+            column = column_window(window_ref, block)
+            total_ref[column] = total_ref[column] + summed
         return carry
 
     lax.fori_loop(0, BLK_DEV // unrolled, one_group, 0)
@@ -270,9 +320,10 @@
         out_shape=(
             jax.ShapeDtypeStruct((N_SRC, BAND_ROWS, OBS), F32),
             jax.ShapeDtypeStruct((BLK_DEV, OBS), F32),
+            jax.ShapeDtypeStruct((1, CODES), jnp.int32),
         ),
-        in_specs=[VMEM] * 5 + [SMEM] * 2,
-        out_specs=(VMEM, VMEM),
+        in_specs=[VMEM] * 6 + [SMEM] * 2,
+        out_specs=(VMEM, VMEM, VMEM),
         scratch_shapes=[
             pltpu.VMEM((BLK_DEV * 8, OBS), F32),
             pltpu.VMEM((len(PAIRS), BLK_DEV, OBS), F32),
@@ -282,7 +333,7 @@
         compiler_params=params(32),
         cost_estimate=pl.CostEstimate(flops=3_000_000_000, bytes_accessed=4_000_000, transcendentals=0),
         name="normal_sums",
-    )(comps, phase, knots, weight, lists, counts, window)
+    )(comps, phase, knots, weight, lists, window.reshape(1, BLK_DEV), counts, window)
 
 
 def solve_five(totals):
@@ -330,7 +381,7 @@
     phase_ref,
     knot_ref,
     source_ref,
-    window_ref,
+    code_ref,
     bands_ref,
     step_ref,
     first_ref,
@@ -368,28 +419,29 @@
                 term_ref[pl.ds(group * 128 + 4 * m + p, 8, stride=16), :] = scaled * comps[p]
         return carry
 
-    lax.fori_loop(0, BLK_DEV // 8, prepare, 0, unroll=8)
+    lax.fori_loop(0, BLK_DEV // 8, prepare, 0, unroll=16)
     total_ref[...] = jnp.zeros_like(total_ref)
-    knot_iota = iota((KNOTS, OBS), 0)
-    unrolled = 64
+    unrolled = 136
 
     def one_group(group, carry):
         for i in range(unrolled):
-            block = group * unrolled + i
-            terms = term_ref[pl.ds(pl.multiple_of(block * 16, 16), 16), :]
-            high, low = split2(terms)
-            hot = (knot_iota == knot_ref[pl.ds(block, 1), :]).astype(F32).astype(BF16)
+            at, blocks = pair_members(code_ref, group * unrolled + i)
+            sides = []
+            for block, offset in blocks:
+                terms = term_ref[pl.ds(pl.multiple_of(block * 16, 16), 16), :]
+                sides.append(
+                    (jnp.concatenate(split2(terms), axis=0), knots_hot(knot_ref, block, offset))
+                )
             summed = lax.dot_general(
-                jnp.concatenate([high, low], axis=1),
-                jnp.concatenate([hot, hot], axis=1),
+                jnp.concatenate([sides[0][0], sides[1][0]], axis=1),
+                jnp.concatenate([sides[0][1], sides[1][1]], axis=1),
                 NT,
                 preferred_element_type=F32,
             )
-            at = column_window(window_ref, block)
-            total_ref[at] = total_ref[at] + summed
+            total_ref[at] = total_ref[at] + (summed[:RIGHT_ROWS] + summed[RIGHT_ROWS:])
         return carry
 
-    lax.fori_loop(0, BLK_DEV // unrolled, one_group, 0)
+    lax.fori_loop(0, N_PAIR // unrolled, one_group, 0)
     for owner in range(N_SRC):
         joined = jnp.concatenate([total_ref[2 * owner], total_ref[2 * owner + 1]], axis=1)
         right = joined[:4]
@@ -399,7 +451,7 @@
         sums_ref[owner, BAND_ROWS:, :] = jnp.concatenate([right, jnp.zeros((4, OBS), F32)], axis=0)
 
 
-def right_sums(parts, design, resid, watt, comps, phase, knots, source_row, window, sums):
+def right_sums(parts, design, resid, watt, comps, phase, knots, source_row, codes, sums):
     return pl.pallas_call(
         rights_kernel,
         out_shape=(
@@ -416,7 +468,7 @@
         ],
         compiler_params=params(32),
         name="right_sums",
-    )(*parts, design, resid, watt, comps, phase, knots, source_row, window, sums)
+    )(*parts, design, resid, watt, comps, phase, knots, source_row, codes, sums)
 
 
 def solve_kernel(prior, got_ref, out_ref, work_ref):
@@ -596,42 +648,67 @@
     )(got)
 
 
-def final_kernel(panel_ref, comp_ref, phase_ref, knot_ref, first_ref, window_ref, out_ref, table_ref):
-    for owner in range(N_SRC):
-        tile = panel_ref[owner]
-        table_ref[owner * 16 : owner * 16 + 8, :] = tile
-        table_ref[owner * 16 + 8 : owner * 16 + 16, :] = roll(tile, 64, 1)
+def window_hot_kernel(window_ref, hot_ref):
+    window = window_ref[...]
+    place = jnp.bitwise_and(window, 1) * N_SRC + lax.shift_right_logical(window, 4)
+    row = iota((OBS, BLK_DEV), 0)
+    hot = (jnp.bitwise_and(row, N_COL - 1) == place) & (row < 3 * N_COL)
+    hot_ref[...] = hot.astype(F32).T
+
+
+def window_hot(window_row):
+    return pl.pallas_call(
+        window_hot_kernel,
+        out_shape=pltpu.VMEM((BLK_DEV, OBS), F32),
+        in_specs=[VMEM],
+        out_specs=VMEM,
+        compiler_params=params(16),
+        name="window_hot",
+    )(window_row)
+
+
+def final_kernel(panel_ref, hot_ref, comp_ref, phase_ref, knot_ref, first_ref, out_ref, table_ref):
+    sides = []
+    for p in range(4):
+        even = panel_ref[pl.ds(p, N_SRC, stride=8), :]
+        sides.append(jnp.concatenate([even, roll(even, KNOTS, 1)], axis=0))
+    pieces = list(split3(jnp.concatenate(sides, axis=1)))
+    pieces = jnp.concatenate(pieces + [jnp.zeros((N_COL, 4 * OBS), BF16)], axis=0)
+    for start in range(0, BLK_DEV, OBS):
+        table_ref[start : start + OBS, :] = jnp.dot(
+            hot_ref[start : start + OBS, :].astype(BF16), pieces, preferred_element_type=F32
+        )
 
     def one_group(group, carry):
         at = pl.ds(pl.multiple_of(group * 8, 8), 8)
         knots = knot_ref[at, :]
         spline = spline_weights(phase_ref[at, :])
-        starts = [column_window(window_ref, group * 8 + i) * 8 for i in range(8)]
         correction = [jnp.zeros((8, OBS), F32) for _ in range(4)]
         for p in range(4):
-            table = jnp.concatenate([table_ref[pl.ds(start + p, 1), :] for start in starts], axis=0)
+            table = table_ref[at, p * OBS : (p + 1) * OBS]
             comps = comp_ref[pl.ds(group * 32 + p, 8, stride=4), :]
             for m in range(4):
-                correction[m] = correction[m] + comps * jnp.take_along_axis(table, knots + m, axis=1)
+                picked = jnp.take_along_axis(table, knots + m, axis=1, mode="promise_in_bounds")
+                correction[m] = correction[m] + comps * picked
         total = spline[0] * correction[0]
         for m in range(1, 4):
             total = total + spline[m] * correction[m]
         out_ref[at, :] = first_ref[at, :] - total
         return carry
 
-    lax.fori_loop(0, BLK_DEV // 8, one_group, 0, unroll=16)
-
-
-def final_residual(panels, comps, phase, knots, first, window):
+    lax.fori_loop(0, BLK_DEV // 8, one_group, 0, unroll=64)
+
+
+def final_residual(panels, hot, comps, phase, knots, first):
     return pl.pallas_call(
         final_kernel,
         out_shape=jax.ShapeDtypeStruct((BLK_DEV, OBS), F32),
-        in_specs=[VMEM] * 5 + [SMEM],
+        in_specs=[VMEM] * 6,
         out_specs=VMEM,
-        scratch_shapes=[pltpu.VMEM((N_COL * 8, OBS), F32)],
+        scratch_shapes=[pltpu.VMEM((BLK_DEV, 4 * OBS), F32)],
         compiler_params=params(16),
         name="final_residual",
-    )(panels, comps, phase, knots, first, window)
+    )(panels.reshape(N_SRC * 8, OBS), hot, comps, phase, knots, first)
 
 
 def shards(
@@ -660,7 +737,7 @@
     stats = source_sums(design, obs_weight, residual, source_row)
     stats = stats + swap(stats, 1)
     parts = (stats, swap(stats, 2), swap(stats, 4), swap(stats, 6))
-    sums, watt = normal_sums(
+    sums, watt, codes = normal_sums(
         comps, spline_phase, knot_offset, obs_weight, send_list, send_count, block_window
     )
     source_step, first, sums = right_sums(
@@ -672,7 +749,7 @@
         spline_phase,
         knot_offset,
         source_row,
-        block_window,
+        codes,
         sums,
     )
     got = lax.all_to_all(sums, "src", split_axis=0, concat_axis=0, tiled=True)
@@ -681,7 +758,8 @@
     attitude_step = (
         own_panels[0, :4].reshape(4, WIN_SUB, KNOTS).transpose(1, 2, 0).reshape(WIN_SUB, KNOTS * 4)
     )
-    last = final_residual(panels, comps, spline_phase, knot_offset, first, block_window)
+    hot = window_hot(block_window.reshape(1, BLK_DEV))
+    last = final_residual(panels, hot, comps, spline_phase, knot_offset, first)
     return (source_step, attitude_step, last)
 
 

time: 66.3 us -> 61.5 us (0.928)
  Pallas kernels: 30.1 us -> 25.9 us
  other arithmetic: 0.74 us -> 0.01 us
    pallas_call x1, Pallas kernels: 8.88 us -> 6.18 us  [right_sums(): pl.pallas_call(rights_kernel, out_shape=(jax.ShapeDtypeStruct((5, SRC_DEV...]
    add x1, other arithmetic: 0.74 us -> 0.01 us  [shards(): stats = stats + swap(stats, 1)]
    pallas_call x1, Pallas kernels: 4.54 us -> 3.84 us  [final_residual(): pl.pallas_call(final_kernel, out_shape=jax.ShapeDtypeStruct((BLK_DEV, OBS...]
    pallas_call x1 -> x2, Pallas kernels: 4.54 us -> 4.03 us  [the longest x1 3.93 us: source_sums(): pl.pallas_call(stats_kernel, out_shape=pltpu.VMEM((STAT_ROWS, SRC_DEV), F...]
where the time goes in v3:
time: 61.5 us; the launch traced here: 61.2 us
  Pallas kernels  25.9 us (42%)
  blocking collectives  17.2 us (28%)
  starting transfers between devices  8.5 us (14%)
  waiting for transfers between devices  7.25 us (12%)
  local copies, waits for them, and re-layouts  1.54 us (3%)
  between operations  0.83 us (1%)
    all_to_all x1, blocking collectives, shards(): got = lax.all_to_all(sums, 'src', split_axis=0, concat_axis=0, tiled=True)  17.2 us
    pallas_call x1, Pallas kernels, normal_sums(): pl.pallas_call(normals_kernel, out_shape=(jax.ShapeDtypeStruct((N_SRC, BA...  8.71 us
    pallas_call x1, Pallas kernels, right_sums(): pl.pallas_call(rights_kernel, out_shape=(jax.ShapeDtypeStruct((5, SRC_DEV...  6.18 us
    all_to_all x1, waiting for transfers between devices, shards(): lax.all_to_all(own_panels, 'src', split_axis=0, concat_axis=0, tiled=True)  6.06 us
    ppermute x4, starting transfers between devices, swap(): return lax.ppermute(values, 'win', [(i, i ^ bit) for i in range(n_win)])  4.78 us
    pallas_call x1, Pallas kernels, source_sums(): pl.pallas_call(stats_kernel, out_shape=pltpu.VMEM((STAT_ROWS, SRC_DEV), F...  3.93 us
    pallas_call x1, Pallas kernels, final_residual(): pl.pallas_call(final_kernel, out_shape=jax.ShapeDtypeStruct((BLK_DEV, OBS...  3.84 us
    all_to_all x1, starting transfers between devices, shards(): lax.all_to_all(own_panels, 'src', split_axis=0, concat_axis=0, tiled=True)  3.71 us
  transfers between devices with their start and end apart: 5, of which 2 were waited for; matrix products, arithmetic and copies ran while one was open for 2% of the time, Pallas kernels for 14%

profile of v3, /device:TPU:0, one launch (start us, length us, event | category | flops | bytes accessed | tf_op | source)
XLA Modules:
  0.0 61.2 jit_solution(1381778303499422417)
XLA Ops:
  0.7 3.9 %source_sums.1 = f32[24,256]{1,0:T(8,128)S(1)} custom-call(f32[5,512,128]{2,1,0:T(8,128)} %bitcast.8, f32[512,128]{1,0:T(8,128)} %weight_ref.1, f32[512,128]{1,0:T(8,128)} %resid_ref.1, s32[1,512]{1,0:T(1,128)} %bitcast.14), custom_call_target="tpu_custom_call" | custom-call | tf_op jit(solution)/shard_map/source_sums/pallas_call | solution.py:127
  4.6 0.1 collective-permute-start
  4.7 1.2 %collective-permute-done = f32[24,256]{1,0:T(8,128)S(1)} collective-permute-done((f32[24,256]{1,0:T(8,128)S(1)}, f32[24,256]{1,0:T(8,128)S(1)}, u32[]{:S(2)}, u32[]{:S(2)}) %collective-permute-start) | collective-permute-done | bytes 24608 | tf_op jit(solution)/shard_map/ppermute | solution.py:735
  5.9 1.6 %collective-permute-start.1 = (f32[24,256]{1,0:T(8,128)S(1)}, f32[24,256]{1,0:T(8,128)S(1)}, u32[]{:S(2)}, u32[]{:S(2)}) collective-permute-start(f32[24,256]{1,0:T(8,128)S(1)} %add.3.own_ref), channel_id=1, source_target_pairs={{0,2},{1,3},{2,0},{3,1},{4,6},{5,7},{6,4},{7,5},{8,10},{9,11},{10,... | collective-permute-start | bytes 73736 | tf_op jit(solution)/shard_map/ppermute | solution.py:735
  7.5 2.7 %collective-permute-start.2 = (f32[24,256]{1,0:T(8,128)S(1)}, f32[24,256]{1,0:T(8,128)S(1)}, u32[]{:S(2)}, u32[]{:S(2)}) collective-permute-start(f32[24,256]{1,0:T(8,128)S(1)} %add.3.own_ref), channel_id=1, source_target_pairs={{0,4},{1,5},{2,6},{3,7},{4,0},{5,1},{6,2},{7,3},{8,12},{9,13},{10,... | collective-permute-start | bytes 73736 | tf_op jit(solution)/shard_map/ppermute | solution.py:735
  10.2 0.4 collective-permute-start.3
  10.6 0.0 copy-done.5
  10.7 0.0 copy-start
  10.7 0.0 copy-start.4
  10.7 0.0 copy-start.6
  10.7 8.7 %normal_sums.1 = (f32[16,40,128]{2,1,0:T(8,128)S(1)}, f32[512,128]{1,0:T(8,128)S(1)}, s32[1,384]{1,0:T(1,128)S(1)}) custom-call(f32[2048,128]{1,0:T(8,128)S(1)} %bitcast.10, f32[512,128]{1,0:T(8,128)S(1)} %copy-done.2, s32[512,128]{1,0:T(8,128)S(1)} %copy-done.3, f32[512,128]{1,0:T(8,128)S(1)} %copy-done.5, s32[16,64]{1,0:T(8,128)S(1)} %copy-done.8, ...), custom_call_target="tpu_custom_call" | custom-call | flops 3000000000 | bytes 4000000 | tf_op jit(solution)/shard_map/normal_sums/pallas_call | solution.py:318
  19.4 0.0 collective-permute-done.1.near_ref
  19.4 0.0 collective-permute-done.2.far_ref
  19.4 0.0 collective-permute-done.3.cross_ref
  19.5 6.2 %right_sums.1 = (f32[5,256]{1,0:T(8,128)}, f32[512,128]{1,0:T(8,128)S(1)}, f32[16,48,128]{2,1,0:T(8,128)S(1)}) custom-call(f32[24,256]{1,0:T(8,128)S(1)} %add.3.own_ref, f32[24,256]{1,0:T(8,128)S(1)} %collective-permute-done.1.near_ref, f32[24,256]{1,0:T(8,128)S(1)} %collective-permute-done.2.far_ref, f32[24,256]{1,0:T(8,128)S(1)} %collective-permute-done.3.cross_ref, ...), custom_call_target="tpu_custom_call" | custom-call | tf_op jit(solution)/shard_map/right_sums/pallas_call | solution.py:455
  25.7 17.2 %all_to_all.10.refs_0_ = f32[16,48,128]{2,1,0:T(8,128)S(1)} all-to-all(f32[16,48,128]{2,1,0:T(8,128)S(1)} %get-tuple-element.13), channel_id=1, replica_groups=mesh['src'=16,'win'=8] {'src'}, dimensions={0} | all-to-all | bytes 786432 | tf_op jit(solution)/shard_map/all_to_all | solution.py:755
  42.9 3.1 %solve_panels.1 = f32[16,8,128]{2,1,0:T(8,128)} custom-call(f32[16,48,128]{2,1,0:T(8,128)S(1)} %all_to_all.10.refs_0_), custom_call_target="tpu_custom_call" | custom-call | tf_op jit(solution)/shard_map/solve_panels/pallas_call | solution.py:640
  46.0 3.7 %all-to-all-start.1 = ((f32[16,8,128]{2,1,0:T(8,128)}), f32[16,8,128]{2,1,0:T(8,128)S(1)}, u32[]{:S(2)}, u32[]{:S(2)}) async-start(f32[16,8,128]{2,1,0:T(8,128)} %solve_panels.1), calls=%async_computation.1 | async-start | bytes 131072 | tf_op jit(solution)/shard_map/all_to_all | solution.py:757
  49.7 0.1 window_hot.1.hot_ref
  49.8 0.7 %slice.4 = f32[1,4,128]{2,1,0:T(4,128)S(1)} slice(f32[16,8,128]{2,1,0:T(8,128)} %solve_panels.1), slice={[0:1], [0:4], [0:128]} | slice | bytes 4096 | tf_op jit(solution)/shard_map/slice | solution.py:759
  50.5 0.1 copy.15
  50.6 0.7 %reshape.25 = f32[2,256]{1,0:T(2,128)} reshape(f32[2,64,4]{2,1,0:T(8,128)S(1)} %bitcast.18) | data formatting | bytes 4096 | tf_op jit(solution)/shard_map/reshape | solution.py:759
  51.3 6.1 %all-to-all-done.1 = f32[16,8,128]{2,1,0:T(8,128)S(1)} async-done(((f32[16,8,128]{2,1,0:T(8,128)}), f32[16,8,128]{2,1,0:T(8,128)S(1)}, u32[]{:S(2)}, u32[]{:S(2)}) %all-to-all-start.1) | async-done | bytes 65568 | tf_op jit(solution)/shard_map/all_to_all | solution.py:757
  57.4 3.8 %final_residual.1 = f32[512,128]{1,0:T(8,128)} custom-call(f32[128,128]{1,0:T(8,128)S(1)} %bitcast.13, f32[512,128]{1,0:T(8,128)S(1)} %window_hot.1.hot_ref, f32[2048,128]{1,0:T(8,128)S(1)} %bitcast.12, f32[512,128]{1,0:T(8,128)S(1)} %copy-done.2, s32[512,128]{1,0:T(8,128)S(1)} %copy-done.3, f32[512,128]{1,0:T(8,128)S(1)} %get-tuple-element.14.first_ref), custom_call_target="tpu_custom_call" | custom-call | tf_op jit(solution)/shard_map/final_residual/pallas_call | solution.py:703
  (17 shorter events, 0.0 us)
Async XLA Ops:
  0.6 10.0 %copy-start.5 = (f32[512,128]{1,0:T(8,128)S(1)}, f32[512,128]{1,0:T(8,128)}, u32[]{:S(2)}) copy-start(f32[512,128]{1,0:T(8,128)} %weight_ref.1) | copy-start | bytes 786436
  0.6 10.0 %copy-start.1 = (f32[512,4,128]{2,1,0:T(4,128)S(1)}, f32[512,4,128]{2,1,0:T(4,128)}, u32[]{:S(2)}) copy-start(f32[512,4,128]{2,1,0:T(4,128)} %param.11) | copy-start | bytes 3145732
  0.7 10.0 %copy-start.7 = (s32[512]{0:T(512)S(1)}, s32[512]{0:T(512)}, u32[]{:S(2)}) copy-start(s32[512]{0:T(512)} %window_ref.1) | copy-start | bytes 6148
  0.7 10.0 %copy-start.2 = (f32[512,128]{1,0:T(8,128)S(1)}, f32[512,128]{1,0:T(8,128)}, u32[]{:S(2)}) copy-start(f32[512,128]{1,0:T(8,128)} %phase_ref.5) | copy-start | bytes 786436
  0.7 10.0 %copy-start.3 = (s32[512,128]{1,0:T(8,128)S(1)}, s32[512,128]{1,0:T(8,128)}, u32[]{:S(2)}) copy-start(s32[512,128]{1,0:T(8,128)} %knot_ref.5) | copy-start | bytes 786436
  0.7 10.0 %copy-start.8 = (s32[16,64]{1,0:T(8,128)S(1)}, s32[16,64]{1,0:T(8,128)}, u32[]{:S(2)}) copy-start(s32[16,64]{1,0:T(8,128)} %list_ref.1) | copy-start | bytes 12292
  0.7 10.0 %copy-start.9 = (s32[16]{0:T(128)S(1)}, s32[16]{0:T(128)}, u32[]{:S(2)}) copy-start(s32[16]{0:T(128)} %count_ref.1) | copy-start | bytes 196
  4.6 1.3 %collective-permute-start = (f32[24,256]{1,0:T(8,128)S(1)}, f32[24,256]{1,0:T(8,128)S(1)}, u32[]{:S(2)}, u32[]{:S(2)}) collective-permute-start(f32[24,256]{1,0:T(8,128)S(1)} %source_sums.1), channel_id=1, source_target_pairs={{0,1},{1,0},{2,3},{3,2},{4,5},{5,4},{6,7},{7,6},{8,9},{9,8},{10,11... | collective-permute-start | bytes 73736 | tf_op jit(solution)/shard_map/ppermute | solution.py:735
  5.9 13.5 %collective-permute-start.1 = (f32[24,256]{1,0:T(8,128)S(1)}, f32[24,256]{1,0:T(8,128)S(1)}, u32[]{:S(2)}, u32[]{:S(2)}) collective-permute-start(f32[24,256]{1,0:T(8,128)S(1)} %add.3.own_ref), channel_id=1, source_target_pairs={{0,2},{1,3},{2,0},{3,1},{4,6},{5,7},{6,4},{7,5},{8,10},{9,11},{10,... | collective-permute-start | bytes 73736 | tf_op jit(solution)/shard_map/ppermute | solution.py:735
  7.5 11.9 %collective-permute-start.2 = (f32[24,256]{1,0:T(8,128)S(1)}, f32[24,256]{1,0:T(8,128)S(1)}, u32[]{:S(2)}, u32[]{:S(2)}) collective-permute-start(f32[24,256]{1,0:T(8,128)S(1)} %add.3.own_ref), channel_id=1, source_target_pairs={{0,4},{1,5},{2,6},{3,7},{4,0},{5,1},{6,2},{7,3},{8,12},{9,13},{10,... | collective-permute-start | bytes 73736 | tf_op jit(solution)/shard_map/ppermute | solution.py:735
  10.2 9.2 %collective-permute-start.3 = (f32[24,256]{1,0:T(8,128)S(1)}, f32[24,256]{1,0:T(8,128)S(1)}, u32[]{:S(2)}, u32[]{:S(2)}) collective-permute-start(f32[24,256]{1,0:T(8,128)S(1)} %add.3.own_ref), channel_id=1, source_target_pairs={{0,6},{1,7},{2,4},{3,5},{4,2},{5,3},{6,0},{7,1},{8,14},{9,15},{10,... | collective-permute-start | bytes 73736 | tf_op jit(solution)/shard_map/ppermute | solution.py:735
  10.7 8.8 %copy-start = (f32[512,5,128]{2,0,1:T(8,128)S(1)}, f32[512,5,128]{2,0,1:T(8,128)}, u32[]{:S(2)}) copy-start(f32[512,5,128]{2,0,1:T(8,128)} %param.10) | copy-start | bytes 3932164
  10.7 8.8 %copy-start.4 = (f32[512,128]{1,0:T(8,128)S(1)}, f32[512,128]{1,0:T(8,128)}, u32[]{:S(2)}) copy-start(f32[512,128]{1,0:T(8,128)} %resid_ref.1) | copy-start | bytes 786436
  10.7 8.8 %copy-start.6 = (s32[512]{0:T(512)S(1)}, s32[512]{0:T(512)}, u32[]{:S(2)}) copy-start(s32[512]{0:T(512)} %param.16) | copy-start | bytes 6148
  46.0 11.4 %all-to-all-start.1 = ((f32[16,8,128]{2,1,0:T(8,128)}), f32[16,8,128]{2,1,0:T(8,128)S(1)}, u32[]{:S(2)}, u32[]{:S(2)}) async-start(f32[16,8,128]{2,1,0:T(8,128)} %solve_panels.1), calls=%async_computation.1 | async-start | bytes 131072 | tf_op jit(solution)/shard_map/all_to_all | solution.py:757

commit v4 on v3

--- a/solution.py
+++ b/solution.py
@@ -283,9 +283,9 @@
             pair_ref[i, at, :] = weighted[p] * comps[q]
         return carry
 
-    lax.fori_loop(0, BLK_DEV // 8, prepare, 0, unroll=16)
+    lax.fori_loop(0, BLK_DEV // 8, prepare, 0, unroll=64)
     total_ref[...] = jnp.zeros_like(total_ref)
-    unrolled = 128
+    unrolled = 256
 
     def one_group(group, carry):
         for i in range(unrolled):
@@ -419,9 +419,9 @@
                 term_ref[pl.ds(group * 128 + 4 * m + p, 8, stride=16), :] = scaled * comps[p]
         return carry
 
-    lax.fori_loop(0, BLK_DEV // 8, prepare, 0, unroll=16)
+    lax.fori_loop(0, BLK_DEV // 8, prepare, 0, unroll=64)
     total_ref[...] = jnp.zeros_like(total_ref)
-    unrolled = 136
+    unrolled = 272
 
     def one_group(group, carry):
         for i in range(unrolled):

time: 61.5 us -> 61 us (level)
  no operation moved by 1% of the time
where the time goes in v4:
time: 61 us; the launch traced here: 60.7 us
  Pallas kernels  25.4 us (42%)
  blocking collectives  17.2 us (28%)
  starting transfers between devices  8.5 us (14%)
  waiting for transfers between devices  7.25 us (12%)
  local copies, waits for them, and re-layouts  1.54 us (3%)
  between operations  0.83 us (1%)
    all_to_all x1, blocking collectives, shards(): got = lax.all_to_all(sums, 'src', split_axis=0, concat_axis=0, tiled=True)  17.2 us
    pallas_call x1, Pallas kernels, normal_sums(): pl.pallas_call(normals_kernel, out_shape=(jax.ShapeDtypeStruct((N_SRC, BA...  8.12 us
    pallas_call x1, Pallas kernels, right_sums(): pl.pallas_call(rights_kernel, out_shape=(jax.ShapeDtypeStruct((5, SRC_DEV...  6.29 us
    all_to_all x1, waiting for transfers between devices, shards(): lax.all_to_all(own_panels, 'src', split_axis=0, concat_axis=0, tiled=True)  6.06 us
    ppermute x4, starting transfers between devices, swap(): return lax.ppermute(values, 'win', [(i, i ^ bit) for i in range(n_win)])  4.78 us
    pallas_call x1, Pallas kernels, source_sums(): pl.pallas_call(stats_kernel, out_shape=pltpu.VMEM((STAT_ROWS, SRC_DEV), F...  3.93 us
    pallas_call x1, Pallas kernels, final_residual(): pl.pallas_call(final_kernel, out_shape=jax.ShapeDtypeStruct((BLK_DEV, OBS...  3.84 us
    all_to_all x1, starting transfers between devices, shards(): lax.all_to_all(own_panels, 'src', split_axis=0, concat_axis=0, tiled=True)  3.71 us
  transfers between devices with their start and end apart: 5, of which 2 were waited for; matrix products, arithmetic and copies ran while one was open for 2% of the time, Pallas kernels for 14%

profile of v4, /device:TPU:0, one launch (start us, length us, event | category | flops | bytes accessed | tf_op | source)
XLA Modules:
  0.0 60.7 jit_solution(3328854250035346042)
XLA Ops:
  0.7 3.9 %source_sums.1 = f32[24,256]{1,0:T(8,128)S(1)} custom-call(f32[5,512,128]{2,1,0:T(8,128)} %bitcast.8, f32[512,128]{1,0:T(8,128)} %weight_ref.1, f32[512,128]{1,0:T(8,128)} %resid_ref.1, s32[1,512]{1,0:T(1,128)} %bitcast.14), custom_call_target="tpu_custom_call" | custom-call | tf_op jit(solution)/shard_map/source_sums/pallas_call | solution.py:127
  4.6 0.1 collective-permute-start
  4.7 1.2 %collective-permute-done = f32[24,256]{1,0:T(8,128)S(1)} collective-permute-done((f32[24,256]{1,0:T(8,128)S(1)}, f32[24,256]{1,0:T(8,128)S(1)}, u32[]{:S(2)}, u32[]{:S(2)}) %collective-permute-start) | collective-permute-done | bytes 24608 | tf_op jit(solution)/shard_map/ppermute | solution.py:735
  5.9 1.6 %collective-permute-start.1 = (f32[24,256]{1,0:T(8,128)S(1)}, f32[24,256]{1,0:T(8,128)S(1)}, u32[]{:S(2)}, u32[]{:S(2)}) collective-permute-start(f32[24,256]{1,0:T(8,128)S(1)} %add.3.own_ref), channel_id=1, source_target_pairs={{0,2},{1,3},{2,0},{3,1},{4,6},{5,7},{6,4},{7,5},{8,10},{9,11},{10,... | collective-permute-start | bytes 73736 | tf_op jit(solution)/shard_map/ppermute | solution.py:735
  7.5 2.7 %collective-permute-start.2 = (f32[24,256]{1,0:T(8,128)S(1)}, f32[24,256]{1,0:T(8,128)S(1)}, u32[]{:S(2)}, u32[]{:S(2)}) collective-permute-start(f32[24,256]{1,0:T(8,128)S(1)} %add.3.own_ref), channel_id=1, source_target_pairs={{0,4},{1,5},{2,6},{3,7},{4,0},{5,1},{6,2},{7,3},{8,12},{9,13},{10,... | collective-permute-start | bytes 73736 | tf_op jit(solution)/shard_map/ppermute | solution.py:735
  10.2 0.4 collective-permute-start.3
  10.6 0.0 copy-done.5
  10.7 0.0 copy-start
  10.7 0.0 copy-start.4
  10.7 0.0 copy-start.6
  10.7 8.1 %normal_sums.1 = (f32[16,40,128]{2,1,0:T(8,128)S(1)}, f32[512,128]{1,0:T(8,128)S(1)}, s32[1,384]{1,0:T(1,128)S(1)}) custom-call(f32[2048,128]{1,0:T(8,128)S(1)} %bitcast.10, f32[512,128]{1,0:T(8,128)S(1)} %copy-done.2, s32[512,128]{1,0:T(8,128)S(1)} %copy-done.3, f32[512,128]{1,0:T(8,128)S(1)} %copy-done.5, s32[16,64]{1,0:T(8,128)S(1)} %copy-done.8, ...), custom_call_target="tpu_custom_call" | custom-call | flops 3000000000 | bytes 4000000 | tf_op jit(solution)/shard_map/normal_sums/pallas_call | solution.py:318
  18.8 0.0 collective-permute-done.1.near_ref
  18.8 0.0 collective-permute-done.2.far_ref
  18.9 0.0 collective-permute-done.3.cross_ref
  18.9 6.3 %right_sums.1 = (f32[5,256]{1,0:T(8,128)}, f32[512,128]{1,0:T(8,128)S(1)}, f32[16,48,128]{2,1,0:T(8,128)S(1)}) custom-call(f32[24,256]{1,0:T(8,128)S(1)} %add.3.own_ref, f32[24,256]{1,0:T(8,128)S(1)} %collective-permute-done.1.near_ref, f32[24,256]{1,0:T(8,128)S(1)} %collective-permute-done.2.far_ref, f32[24,256]{1,0:T(8,128)S(1)} %collective-permute-done.3.cross_ref, ...), custom_call_target="tpu_custom_call" | custom-call | tf_op jit(solution)/shard_map/right_sums/pallas_call | solution.py:455
  25.2 17.2 %all_to_all.10.refs_0_ = f32[16,48,128]{2,1,0:T(8,128)S(1)} all-to-all(f32[16,48,128]{2,1,0:T(8,128)S(1)} %get-tuple-element.13), channel_id=1, replica_groups=mesh['src'=16,'win'=8] {'src'}, dimensions={0} | all-to-all | bytes 786432 | tf_op jit(solution)/shard_map/all_to_all | solution.py:755
  42.4 3.1 %solve_panels.1 = f32[16,8,128]{2,1,0:T(8,128)} custom-call(f32[16,48,128]{2,1,0:T(8,128)S(1)} %all_to_all.10.refs_0_), custom_call_target="tpu_custom_call" | custom-call | tf_op jit(solution)/shard_map/solve_panels/pallas_call | solution.py:640
  45.5 3.7 %all-to-all-start.1 = ((f32[16,8,128]{2,1,0:T(8,128)}), f32[16,8,128]{2,1,0:T(8,128)S(1)}, u32[]{:S(2)}, u32[]{:S(2)}) async-start(f32[16,8,128]{2,1,0:T(8,128)} %solve_panels.1), calls=%async_computation.1 | async-start | bytes 131072 | tf_op jit(solution)/shard_map/all_to_all | solution.py:757
  49.2 0.1 window_hot.1.hot_ref
  49.3 0.7 %slice.4 = f32[1,4,128]{2,1,0:T(4,128)S(1)} slice(f32[16,8,128]{2,1,0:T(8,128)} %solve_panels.1), slice={[0:1], [0:4], [0:128]} | slice | bytes 4096 | tf_op jit(solution)/shard_map/slice | solution.py:759
  50.0 0.1 copy.15
  50.2 0.7 %reshape.25 = f32[2,256]{1,0:T(2,128)} reshape(f32[2,64,4]{2,1,0:T(8,128)S(1)} %bitcast.18) | data formatting | bytes 4096 | tf_op jit(solution)/shard_map/reshape | solution.py:759
  50.8 6.1 %all-to-all-done.1 = f32[16,8,128]{2,1,0:T(8,128)S(1)} async-done(((f32[16,8,128]{2,1,0:T(8,128)}), f32[16,8,128]{2,1,0:T(8,128)S(1)}, u32[]{:S(2)}, u32[]{:S(2)}) %all-to-all-start.1) | async-done | bytes 65568 | tf_op jit(solution)/shard_map/all_to_all | solution.py:757
  56.9 3.8 %final_residual.1 = f32[512,128]{1,0:T(8,128)} custom-call(f32[128,128]{1,0:T(8,128)S(1)} %bitcast.13, f32[512,128]{1,0:T(8,128)S(1)} %window_hot.1.hot_ref, f32[2048,128]{1,0:T(8,128)S(1)} %bitcast.12, f32[512,128]{1,0:T(8,128)S(1)} %copy-done.2, s32[512,128]{1,0:T(8,128)S(1)} %copy-done.3, f32[512,128]{1,0:T(8,128)S(1)} %get-tuple-element.14.first_ref), custom_call_target="tpu_custom_call" | custom-call | tf_op jit(solution)/shard_map/final_residual/pallas_call | solution.py:703
  (17 shorter events, 0.0 us)
Async XLA Ops:
  0.6 10.0 %copy-start.5 = (f32[512,128]{1,0:T(8,128)S(1)}, f32[512,128]{1,0:T(8,128)}, u32[]{:S(2)}) copy-start(f32[512,128]{1,0:T(8,128)} %weight_ref.1) | copy-start | bytes 786436
  0.6 10.0 %copy-start.1 = (f32[512,4,128]{2,1,0:T(4,128)S(1)}, f32[512,4,128]{2,1,0:T(4,128)}, u32[]{:S(2)}) copy-start(f32[512,4,128]{2,1,0:T(4,128)} %param.11) | copy-start | bytes 3145732
  0.7 10.0 %copy-start.7 = (s32[512]{0:T(512)S(1)}, s32[512]{0:T(512)}, u32[]{:S(2)}) copy-start(s32[512]{0:T(512)} %window_ref.1) | copy-start | bytes 6148
  0.7 10.0 %copy-start.2 = (f32[512,128]{1,0:T(8,128)S(1)}, f32[512,128]{1,0:T(8,128)}, u32[]{:S(2)}) copy-start(f32[512,128]{1,0:T(8,128)} %phase_ref.5) | copy-start | bytes 786436
  0.7 10.0 %copy-start.3 = (s32[512,128]{1,0:T(8,128)S(1)}, s32[512,128]{1,0:T(8,128)}, u32[]{:S(2)}) copy-start(s32[512,128]{1,0:T(8,128)} %knot_ref.5) | copy-start | bytes 786436
  0.7 10.0 %copy-start.8 = (s32[16,64]{1,0:T(8,128)S(1)}, s32[16,64]{1,0:T(8,128)}, u32[]{:S(2)}) copy-start(s32[16,64]{1,0:T(8,128)} %list_ref.1) | copy-start | bytes 12292
  0.7 10.0 %copy-start.9 = (s32[16]{0:T(128)S(1)}, s32[16]{0:T(128)}, u32[]{:S(2)}) copy-start(s32[16]{0:T(128)} %count_ref.1) | copy-start | bytes 196
  4.6 1.3 %collective-permute-start = (f32[24,256]{1,0:T(8,128)S(1)}, f32[24,256]{1,0:T(8,128)S(1)}, u32[]{:S(2)}, u32[]{:S(2)}) collective-permute-start(f32[24,256]{1,0:T(8,128)S(1)} %source_sums.1), channel_id=1, source_target_pairs={{0,1},{1,0},{2,3},{3,2},{4,5},{5,4},{6,7},{7,6},{8,9},{9,8},{10,11... | collective-permute-start | bytes 73736 | tf_op jit(solution)/shard_map/ppermute | solution.py:735
  5.9 12.9 %collective-permute-start.1 = (f32[24,256]{1,0:T(8,128)S(1)}, f32[24,256]{1,0:T(8,128)S(1)}, u32[]{:S(2)}, u32[]{:S(2)}) collective-permute-start(f32[24,256]{1,0:T(8,128)S(1)} %add.3.own_ref), channel_id=1, source_target_pairs={{0,2},{1,3},{2,0},{3,1},{4,6},{5,7},{6,4},{7,5},{8,10},{9,11},{10,... | collective-permute-start | bytes 73736 | tf_op jit(solution)/shard_map/ppermute | solution.py:735
  7.5 11.3 %collective-permute-start.2 = (f32[24,256]{1,0:T(8,128)S(1)}, f32[24,256]{1,0:T(8,128)S(1)}, u32[]{:S(2)}, u32[]{:S(2)}) collective-permute-start(f32[24,256]{1,0:T(8,128)S(1)} %add.3.own_ref), channel_id=1, source_target_pairs={{0,4},{1,5},{2,6},{3,7},{4,0},{5,1},{6,2},{7,3},{8,12},{9,13},{10,... | collective-permute-start | bytes 73736 | tf_op jit(solution)/shard_map/ppermute | solution.py:735
  10.2 8.6 %collective-permute-start.3 = (f32[24,256]{1,0:T(8,128)S(1)}, f32[24,256]{1,0:T(8,128)S(1)}, u32[]{:S(2)}, u32[]{:S(2)}) collective-permute-start(f32[24,256]{1,0:T(8,128)S(1)} %add.3.own_ref), channel_id=1, source_target_pairs={{0,6},{1,7},{2,4},{3,5},{4,2},{5,3},{6,0},{7,1},{8,14},{9,15},{10,... | collective-permute-start | bytes 73736 | tf_op jit(solution)/shard_map/ppermute | solution.py:735
  10.7 8.2 %copy-start = (f32[512,5,128]{2,0,1:T(8,128)S(1)}, f32[512,5,128]{2,0,1:T(8,128)}, u32[]{:S(2)}) copy-start(f32[512,5,128]{2,0,1:T(8,128)} %param.10) | copy-start | bytes 3932164
  10.7 8.2 %copy-start.4 = (f32[512,128]{1,0:T(8,128)S(1)}, f32[512,128]{1,0:T(8,128)}, u32[]{:S(2)}) copy-start(f32[512,128]{1,0:T(8,128)} %resid_ref.1) | copy-start | bytes 786436
  10.7 8.2 %copy-start.6 = (s32[512]{0:T(512)S(1)}, s32[512]{0:T(512)}, u32[]{:S(2)}) copy-start(s32[512]{0:T(512)} %param.16) | copy-start | bytes 6148
  45.5 11.4 %all-to-all-start.1 = ((f32[16,8,128]{2,1,0:T(8,128)}), f32[16,8,128]{2,1,0:T(8,128)S(1)}, u32[]{:S(2)}, u32[]{:S(2)}) async-start(f32[16,8,128]{2,1,0:T(8,128)} %solve_panels.1), calls=%async_computation.1 | async-start | bytes 131072 | tf_op jit(solution)/shard_map/all_to_all | solution.py:757

commit v5 on v3

--- a/solution.py
+++ b/solution.py
@@ -419,7 +419,7 @@
                 term_ref[pl.ds(group * 128 + 4 * m + p, 8, stride=16), :] = scaled * comps[p]
         return carry
 
-    lax.fori_loop(0, BLK_DEV // 8, prepare, 0, unroll=16)
+    lax.fori_loop(0, BLK_DEV // 8, prepare, 0, unroll=64)
     total_ref[...] = jnp.zeros_like(total_ref)
     unrolled = 136
 
@@ -630,7 +630,7 @@
     from_lane = jnp.where(knot < 32, lane8, window_at + 32 + KNOTS - 1 - knot)
     panel = jnp.take_along_axis(result, from_lane, axis=1)
     for owner in range(N_SRC):
-        out_ref[owner] = panel
+        out_ref[owner] = panel[:4]
 
 
 def solve_panels(got, prior):
@@ -639,7 +639,7 @@
 
     return pl.pallas_call(
         body,
-        out_shape=jax.ShapeDtypeStruct((N_SRC, 8, OBS), F32),
+        out_shape=jax.ShapeDtypeStruct((N_SRC, 4, OBS), F32),
         in_specs=[VMEM],
         out_specs=VMEM,
         scratch_shapes=[pltpu.VMEM((HALF * 13, 8, OBS), F32)],
@@ -670,7 +670,7 @@
 def final_kernel(panel_ref, hot_ref, comp_ref, phase_ref, knot_ref, first_ref, out_ref, table_ref):
     sides = []
     for p in range(4):
-        even = panel_ref[pl.ds(p, N_SRC, stride=8), :]
+        even = panel_ref[pl.ds(p, N_SRC, stride=4), :]
         sides.append(jnp.concatenate([even, roll(even, KNOTS, 1)], axis=0))
     pieces = list(split3(jnp.concatenate(sides, axis=1)))
     pieces = jnp.concatenate(pieces + [jnp.zeros((N_COL, 4 * OBS), BF16)], axis=0)
@@ -708,7 +708,7 @@
         scratch_shapes=[pltpu.VMEM((BLK_DEV, 4 * OBS), F32)],
         compiler_params=params(16),
         name="final_residual",
-    )(panels.reshape(N_SRC * 8, OBS), hot, comps, phase, knots, first)
+    )(panels.reshape(N_SRC * 4, OBS), hot, comps, phase, knots, first)
 
 
 def shards(
@@ -756,7 +756,7 @@
     own_panels = solve_panels(got, prior)
     panels = lax.all_to_all(own_panels, "src", split_axis=0, concat_axis=0, tiled=True)
     attitude_step = (
-        own_panels[0, :4].reshape(4, WIN_SUB, KNOTS).transpose(1, 2, 0).reshape(WIN_SUB, KNOTS * 4)
+        own_panels[0].reshape(4, WIN_SUB, KNOTS).transpose(1, 2, 0).reshape(WIN_SUB, KNOTS * 4)
     )
     hot = window_hot(block_window.reshape(1, BLK_DEV))
     last = final_residual(panels, hot, comps, spline_phase, knot_offset, first)

time: 61.5 us -> 61.2 us (level)
  no operation moved by 1% of the time
where the time goes in v5:
time: 61.2 us; the launch traced here: 60.9 us
  Pallas kernels  25.6 us (42%)
  blocking collectives  17.2 us (28%)
  starting transfers between devices  8.5 us (14%)
  waiting for transfers between devices  7.21 us (12%)
  local copies, waits for them, and re-layouts  1.54 us (3%)
  between operations  0.83 us (1%)
    all_to_all x1, blocking collectives, shards(): got = lax.all_to_all(sums, 'src', split_axis=0, concat_axis=0, tiled=True)  17.2 us
    pallas_call x1, Pallas kernels, normal_sums(): pl.pallas_call(normals_kernel, out_shape=(jax.ShapeDtypeStruct((N_SRC, BA...  8.69 us
    all_to_all x1, waiting for transfers between devices, shards(): lax.all_to_all(own_panels, 'src', split_axis=0, concat_axis=0, tiled=True)  6.02 us
    pallas_call x1, Pallas kernels, right_sums(): pl.pallas_call(rights_kernel, out_shape=(jax.ShapeDtypeStruct((5, SRC_DEV...  5.94 us
    ppermute x4, starting transfers between devices, swap(): return lax.ppermute(values, 'win', [(i, i ^ bit) for i in range(n_win)])  4.78 us
    pallas_call x1, Pallas kernels, source_sums(): pl.pallas_call(stats_kernel, out_shape=pltpu.VMEM((STAT_ROWS, SRC_DEV), F...  3.93 us
    pallas_call x1, Pallas kernels, final_residual(): pl.pallas_call(final_kernel, out_shape=jax.ShapeDtypeStruct((BLK_DEV, OBS...  3.84 us
    all_to_all x1, starting transfers between devices, shards(): lax.all_to_all(own_panels, 'src', split_axis=0, concat_axis=0, tiled=True)  3.71 us
  transfers between devices with their start and end apart: 5, of which 2 were waited for; matrix products, arithmetic and copies ran while one was open for 2% of the time, Pallas kernels for 14%

profile of v5, /device:TPU:0, one launch (start us, length us, event | category | flops | bytes accessed | tf_op | source)
XLA Modules:
  0.0 60.9 jit_solution(8964372514628732911)
XLA Ops:
  0.6 0.0 copy-start.5
  0.7 3.9 %source_sums.1 = f32[24,256]{1,0:T(8,128)S(1)} custom-call(f32[5,512,128]{2,1,0:T(8,128)} %bitcast.8, f32[512,128]{1,0:T(8,128)} %weight_ref.1, f32[512,128]{1,0:T(8,128)} %resid_ref.1, s32[1,512]{1,0:T(1,128)} %bitcast.14), custom_call_target="tpu_custom_call" | custom-call | tf_op jit(solution)/shard_map/source_sums/pallas_call | solution.py:127
  4.6 0.1 collective-permute-start
  4.7 1.2 %collective-permute-done = f32[24,256]{1,0:T(8,128)S(1)} collective-permute-done((f32[24,256]{1,0:T(8,128)S(1)}, f32[24,256]{1,0:T(8,128)S(1)}, u32[]{:S(2)}, u32[]{:S(2)}) %collective-permute-start) | collective-permute-done | bytes 24608 | tf_op jit(solution)/shard_map/ppermute | solution.py:735
  5.9 1.6 %collective-permute-start.1 = (f32[24,256]{1,0:T(8,128)S(1)}, f32[24,256]{1,0:T(8,128)S(1)}, u32[]{:S(2)}, u32[]{:S(2)}) collective-permute-start(f32[24,256]{1,0:T(8,128)S(1)} %add.3.own_ref), channel_id=1, source_target_pairs={{0,2},{1,3},{2,0},{3,1},{4,6},{5,7},{6,4},{7,5},{8,10},{9,11},{10,... | collective-permute-start | bytes 73736 | tf_op jit(solution)/shard_map/ppermute | solution.py:735
  7.5 2.7 %collective-permute-start.2 = (f32[24,256]{1,0:T(8,128)S(1)}, f32[24,256]{1,0:T(8,128)S(1)}, u32[]{:S(2)}, u32[]{:S(2)}) collective-permute-start(f32[24,256]{1,0:T(8,128)S(1)} %add.3.own_ref), channel_id=1, source_target_pairs={{0,4},{1,5},{2,6},{3,7},{4,0},{5,1},{6,2},{7,3},{8,12},{9,13},{10,... | collective-permute-start | bytes 73736 | tf_op jit(solution)/shard_map/ppermute | solution.py:735
  10.2 0.4 collective-permute-start.3
  10.7 0.0 copy-start
  10.7 0.0 copy-start.4
  10.7 0.0 copy-start.6
  10.7 8.7 %normal_sums.1 = (f32[16,40,128]{2,1,0:T(8,128)S(1)}, f32[512,128]{1,0:T(8,128)S(1)}, s32[1,384]{1,0:T(1,128)S(1)}) custom-call(f32[2048,128]{1,0:T(8,128)S(1)} %bitcast.10, f32[512,128]{1,0:T(8,128)S(1)} %copy-done.2, s32[512,128]{1,0:T(8,128)S(1)} %copy-done.3, f32[512,128]{1,0:T(8,128)S(1)} %copy-done.5, s32[16,64]{1,0:T(8,128)S(1)} %copy-done.8, ...), custom_call_target="tpu_custom_call" | custom-call | flops 3000000000 | bytes 4000000 | tf_op jit(solution)/shard_map/normal_sums/pallas_call | solution.py:318
  19.4 0.0 collective-permute-done.1.near_ref
  19.4 0.0 collective-permute-done.2.far_ref
  19.4 0.0 collective-permute-done.3.cross_ref
  19.5 5.9 %right_sums.1 = (f32[5,256]{1,0:T(8,128)}, f32[512,128]{1,0:T(8,128)S(1)}, f32[16,48,128]{2,1,0:T(8,128)S(1)}) custom-call(f32[24,256]{1,0:T(8,128)S(1)} %add.3.own_ref, f32[24,256]{1,0:T(8,128)S(1)} %collective-permute-done.1.near_ref, f32[24,256]{1,0:T(8,128)S(1)} %collective-permute-done.2.far_ref, f32[24,256]{1,0:T(8,128)S(1)} %collective-permute-done.3.cross_ref, ...), custom_call_target="tpu_custom_call" | custom-call | tf_op jit(solution)/shard_map/right_sums/pallas_call | solution.py:455
  25.4 17.2 %all_to_all.10.refs_0_ = f32[16,48,128]{2,1,0:T(8,128)S(1)} all-to-all(f32[16,48,128]{2,1,0:T(8,128)S(1)} %get-tuple-element.13), channel_id=1, replica_groups=mesh['src'=16,'win'=8] {'src'}, dimensions={0} | all-to-all | bytes 786432 | tf_op jit(solution)/shard_map/all_to_all | solution.py:755
  42.6 3.1 %solve_panels.1 = f32[16,4,128]{2,1,0:T(4,128)} custom-call(f32[16,48,128]{2,1,0:T(8,128)S(1)} %all_to_all.10.refs_0_), custom_call_target="tpu_custom_call" | custom-call | tf_op jit(solution)/shard_map/solve_panels/pallas_call | solution.py:640
  45.7 3.7 %all-to-all-start.1 = ((f32[16,4,128]{2,1,0:T(4,128)}), f32[16,4,128]{2,1,0:T(4,128)S(1)}, u32[]{:S(2)}, u32[]{:S(2)}) async-start(f32[16,4,128]{2,1,0:T(4,128)} %solve_panels.1), calls=%async_computation.1 | async-start | bytes 65536 | tf_op jit(solution)/shard_map/all_to_all | solution.py:757
  49.5 0.1 window_hot.1.hot_ref
  49.6 0.7 %slice.4 = f32[1,4,128]{2,1,0:T(4,128)S(1)} slice(f32[16,4,128]{2,1,0:T(4,128)} %solve_panels.1), slice={[0:1], [0:4], [0:128]} | slice | bytes 4096 | tf_op jit(solution)/shard_map/slice | solution.py:759
  50.3 0.1 copy.15
  50.4 0.7 %reshape.25 = f32[2,256]{1,0:T(2,128)} reshape(f32[2,64,4]{2,1,0:T(8,128)S(1)} %bitcast.18) | data formatting | bytes 4096 | tf_op jit(solution)/shard_map/reshape | solution.py:759
  51.1 6.0 %all-to-all-done.1 = f32[16,4,128]{2,1,0:T(4,128)S(1)} async-done(((f32[16,4,128]{2,1,0:T(4,128)}), f32[16,4,128]{2,1,0:T(4,128)S(1)}, u32[]{:S(2)}, u32[]{:S(2)}) %all-to-all-start.1) | async-done | bytes 32800 | tf_op jit(solution)/shard_map/all_to_all | solution.py:757
  57.1 3.8 %final_residual.1 = f32[512,128]{1,0:T(8,128)} custom-call(f32[64,128]{1,0:T(8,128)S(1)} %bitcast.13, f32[512,128]{1,0:T(8,128)S(1)} %window_hot.1.hot_ref, f32[2048,128]{1,0:T(8,128)S(1)} %bitcast.12, f32[512,128]{1,0:T(8,128)S(1)} %copy-done.2, s32[512,128]{1,0:T(8,128)S(1)} %copy-done.3, f32[512,128]{1,0:T(8,128)S(1)} %get-tuple-element.14.first_ref), custom_call_target="tpu_custom_call" | custom-call | tf_op jit(solution)/shard_map/final_residual/pallas_call | solution.py:703
  (17 shorter events, 0.0 us)
Async XLA Ops:
  0.6 10.0 %copy-start.5 = (f32[512,128]{1,0:T(8,128)S(1)}, f32[512,128]{1,0:T(8,128)}, u32[]{:S(2)}) copy-start(f32[512,128]{1,0:T(8,128)} %weight_ref.1) | copy-start | bytes 786436
  0.6 10.0 %copy-start.1 = (f32[512,4,128]{2,1,0:T(4,128)S(1)}, f32[512,4,128]{2,1,0:T(4,128)}, u32[]{:S(2)}) copy-start(f32[512,4,128]{2,1,0:T(4,128)} %param.11) | copy-start | bytes 3145732
  0.7 10.0 %copy-start.7 = (s32[512]{0:T(512)S(1)}, s32[512]{0:T(512)}, u32[]{:S(2)}) copy-start(s32[512]{0:T(512)} %window_ref.1) | copy-start | bytes 6148
  0.7 10.0 %copy-start.2 = (f32[512,128]{1,0:T(8,128)S(1)}, f32[512,128]{1,0:T(8,128)}, u32[]{:S(2)}) copy-start(f32[512,128]{1,0:T(8,128)} %phase_ref.5) | copy-start | bytes 786436
  0.7 10.0 %copy-start.3 = (s32[512,128]{1,0:T(8,128)S(1)}, s32[512,128]{1,0:T(8,128)}, u32[]{:S(2)}) copy-start(s32[512,128]{1,0:T(8,128)} %knot_ref.5) | copy-start | bytes 786436
  0.7 10.0 %copy-start.8 = (s32[16,64]{1,0:T(8,128)S(1)}, s32[16,64]{1,0:T(8,128)}, u32[]{:S(2)}) copy-start(s32[16,64]{1,0:T(8,128)} %list_ref.1) | copy-start | bytes 12292
  0.7 10.0 %copy-start.9 = (s32[16]{0:T(128)S(1)}, s32[16]{0:T(128)}, u32[]{:S(2)}) copy-start(s32[16]{0:T(128)} %count_ref.1) | copy-start | bytes 196
  4.6 1.3 %collective-permute-start = (f32[24,256]{1,0:T(8,128)S(1)}, f32[24,256]{1,0:T(8,128)S(1)}, u32[]{:S(2)}, u32[]{:S(2)}) collective-permute-start(f32[24,256]{1,0:T(8,128)S(1)} %source_sums.1), channel_id=1, source_target_pairs={{0,1},{1,0},{2,3},{3,2},{4,5},{5,4},{6,7},{7,6},{8,9},{9,8},{10,11... | collective-permute-start | bytes 73736 | tf_op jit(solution)/shard_map/ppermute | solution.py:735
  5.9 13.5 %collective-permute-start.1 = (f32[24,256]{1,0:T(8,128)S(1)}, f32[24,256]{1,0:T(8,128)S(1)}, u32[]{:S(2)}, u32[]{:S(2)}) collective-permute-start(f32[24,256]{1,0:T(8,128)S(1)} %add.3.own_ref), channel_id=1, source_target_pairs={{0,2},{1,3},{2,0},{3,1},{4,6},{5,7},{6,4},{7,5},{8,10},{9,11},{10,... | collective-permute-start | bytes 73736 | tf_op jit(solution)/shard_map/ppermute | solution.py:735
  7.5 11.9 %collective-permute-start.2 = (f32[24,256]{1,0:T(8,128)S(1)}, f32[24,256]{1,0:T(8,128)S(1)}, u32[]{:S(2)}, u32[]{:S(2)}) collective-permute-start(f32[24,256]{1,0:T(8,128)S(1)} %add.3.own_ref), channel_id=1, source_target_pairs={{0,4},{1,5},{2,6},{3,7},{4,0},{5,1},{6,2},{7,3},{8,12},{9,13},{10,... | collective-permute-start | bytes 73736 | tf_op jit(solution)/shard_map/ppermute | solution.py:735
  10.2 9.2 %collective-permute-start.3 = (f32[24,256]{1,0:T(8,128)S(1)}, f32[24,256]{1,0:T(8,128)S(1)}, u32[]{:S(2)}, u32[]{:S(2)}) collective-permute-start(f32[24,256]{1,0:T(8,128)S(1)} %add.3.own_ref), channel_id=1, source_target_pairs={{0,6},{1,7},{2,4},{3,5},{4,2},{5,3},{6,0},{7,1},{8,14},{9,15},{10,... | collective-permute-start | bytes 73736 | tf_op jit(solution)/shard_map/ppermute | solution.py:735
  10.7 8.8 %copy-start = (f32[512,5,128]{2,0,1:T(8,128)S(1)}, f32[512,5,128]{2,0,1:T(8,128)}, u32[]{:S(2)}) copy-start(f32[512,5,128]{2,0,1:T(8,128)} %param.10) | copy-start | bytes 3932164
  10.7 8.8 %copy-start.4 = (f32[512,128]{1,0:T(8,128)S(1)}, f32[512,128]{1,0:T(8,128)}, u32[]{:S(2)}) copy-start(f32[512,128]{1,0:T(8,128)} %resid_ref.1) | copy-start | bytes 786436
  10.7 8.8 %copy-start.6 = (s32[512]{0:T(512)S(1)}, s32[512]{0:T(512)}, u32[]{:S(2)}) copy-start(s32[512]{0:T(512)} %param.16) | copy-start | bytes 6148
  45.7 11.3 %all-to-all-start.1 = ((f32[16,4,128]{2,1,0:T(4,128)}), f32[16,4,128]{2,1,0:T(4,128)S(1)}, u32[]{:S(2)}, u32[]{:S(2)}) async-start(f32[16,4,128]{2,1,0:T(4,128)} %solve_panels.1), calls=%async_computation.1 | async-start | bytes 65536 | tf_op jit(solution)/shard_map/all_to_all | solution.py:757
